TPU v7x, 256 devices: a whole 4x4x8 slice. The times are simulated.
256 devices in a mesh: unit: 16 (over x_lo, y, core), feat: 8 (over z), tm: 2 (over x_hi).
Axes of the slice: x: 4 (x_hi: 2, x_lo: 2; x = x_hi * 2 + x_lo), y: 4, z: 8, core: 2. Of those that a mesh axis runs over, the one named last changes fastest.
Arguments:
- tensor: bfloat16 [32, 16384, 2048], P('tm', 'unit', 'feat'), may hold values from -6 to 6
- unit_factor: float32 [16384, 64], P(('unit', 'feat', 'tm')), may hold values from -0.32 to 0.32
- window_factor: float32 [32, 64], P('tm'), may hold values from -1.5 to 1.5
- feat_factor: float32 [2048, 64], P(('feat', 'tm')), may hold values from -0.32 to 0.32
Outputs:
- grad_unit: float32 [16384, 64], P(('unit', 'feat', 'tm'))
- grad_window: float32 [32, 64], P('tm')
- grad_feat: float32 [2048, 64], P(('feat', 'tm'))
All inputs are finite; a program needn't handle non-finite values.
Results may differ from a plain program's by a relative error of at most 0.0065.
Values may be sent and summed in bfloat16 or wider, within the bound.
No kernel may reach another device: no remote copies, remote signals or barrier semaphores. Data moves between devices by JAX's collectives and lax.ppermute only.
A program may use at most 64 MiB of HBM per device.

v0:
```python
import math

import jax
import jax.numpy as jnp
from jax import lax
from jax.sharding import PartitionSpec as P


def body(tensor, unit_factor, window_factor, feat_factor):
    high = lax.Precision.HIGHEST
    win_rows, unit_count, feat_count = tensor.shape
    units_all = unit_count * lax.axis_size("unit")
    windows_all = win_rows * lax.axis_size("tm")
    feats_all = feat_count * lax.axis_size("feat")
    window_wide = window_factor.astype(jnp.bfloat16).astype(jnp.float32)
    feat_low = lax.all_gather(feat_factor.astype(jnp.bfloat16), "tm", axis=0, tiled=True)
    first = jnp.einsum("jik,kr->jir", tensor, feat_low, preferred_element_type=jnp.float32)
    piece = lax.all_gather(unit_factor.astype(jnp.bfloat16), ("feat", "tm"), axis=0, tiled=True)
    second = jnp.einsum("jik,ir->jkr", tensor, piece, preferred_element_type=jnp.float32)
    rows_first = first
    window_part = jnp.einsum("jir,ir->jr", rows_first, piece.astype(jnp.float32))
    second, window_part = (second, window_part)
    rows_first = first
    by_unit = lax.psum_scatter(
        jnp.einsum("jir,jr->ir", rows_first, window_wide),
        ("feat", "tm"),
        scatter_dimension=0,
        tiled=True,
    )
    by_window = lax.psum(window_part, ("unit", "feat"))
    feat_term = jnp.einsum("jkr,jr->kr", second, window_wide)
    half_rows = feat_factor.shape[0]
    feat_full = lax.psum(feat_term, ("unit", "tm"))
    by_feat = lax.dynamic_slice_in_dim(feat_full, lax.axis_index("tm") * half_rows, half_rows, 0)
    unit_gram_part = jnp.dot(
        unit_factor.T, unit_factor, precision=high, preferred_element_type=jnp.float32
    )
    window_gram_part = jnp.dot(
        window_factor.T, window_factor, precision=high, preferred_element_type=jnp.float32
    )
    feat_gram_part = jnp.dot(
        feat_factor.T, feat_factor, precision=high, preferred_element_type=jnp.float32
    )
    gram_unit = lax.psum(unit_gram_part, ("unit", "feat", "tm"))
    gram_window = lax.psum(window_gram_part, "tm")
    gram_feat = lax.psum(feat_gram_part, ("feat", "tm"))
    grad_unit = (
        jnp.dot(
            unit_factor, gram_window * gram_feat, precision=high, preferred_element_type=jnp.float32
        )
        - by_unit
    ) / math.sqrt(windows_all * feats_all)
    grad_window = (
        jnp.dot(
            window_factor, gram_unit * gram_feat, precision=high, preferred_element_type=jnp.float32
        )
        - by_window
    ) / math.sqrt(units_all * feats_all)
    grad_feat = (
        jnp.dot(
            feat_factor, gram_unit * gram_window, precision=high, preferred_element_type=jnp.float32
        )
        - by_feat
    ) / math.sqrt(units_all * windows_all)
    return (grad_unit, grad_window, grad_feat)


def solution(mesh):
    in_specs = (
        P("tm", "unit", "feat"),
        P(("unit", "feat", "tm"), None),
        P("tm", None),
        P(("feat", "tm"), None),
    )
    out_specs = (P(("unit", "feat", "tm"), None), P("tm", None), P(("feat", "tm"), None))
    return jax.shard_map(body, mesh=mesh, in_specs=in_specs, out_specs=out_specs, check_vma=False)
```

profile of v0, /device:TPU:2, one launch (start us, length us, event | category | flops | bytes accessed | tf_op | source)
XLA Modules:
  0.0 524.9 jit_solution(8104831306827771799)
XLA Ops:
  8.0 0.0 all-reduce.2.cloned.1.call-start
  8.0 0.8 convert_element_type.13
  8.8 44.4 %all_gather.7 = bf16[1024,64]{1,0:T(8,128)(2,1)S(1)} all-gather(bf16[64,64]{1,0:T(8,128)(2,1)S(1)} %convert_element_type.13), channel_id=1, replica_groups=mesh['unit'=16,'feat'=8,'tm'=2] {'feat','tm'}, dimensions={0}, use_global_device_ids=true | all-gather | bytes 139264 | tf_op jit(solution)/shard_map/all_gather | solution.py:18
  53.2 0.7 bitcast_convert_fusion.1
  53.9 0.0 copy-start
  53.9 5.8 %multiply_reduce_fusion.1 = f32[64,256]{0,1:T(8,128)S(1)} fusion(bf16[16,1024,256]{2,1,0:T(8,128)(2,1)} %param.4, f32[64,16]{0,1:T(8,128)S(1)} %get-tuple-element.9, bf16[1024,64]{1,0:T(8,128)(2,1)S(1)} %all_gather.7), kind=kOutput, calls=%fused_computation.3 | convolution fusion | flops 537378816 | bytes 8589312 | tf_op jit(solution)/shard_map/jik,ir->jkr/dot_general | solution.py:19
  59.7 0.7 copy.22
  60.4 0.0 all-reduce.2.cloned.1.call-update
  60.4 0.0 reduce-scatter.4.cloned.1.call-start
  60.5 0.2 copy.26
  60.7 0.0 copy-done
  60.7 5.9 %all_gather.6 = bf16[256,64]{0,1:T(8,128)(2,1)S(1)} all-gather(bf16[128,64]{0,1:T(8,128)(2,1)S(1)} %convert_element_type.11), channel_id=1, replica_groups=mesh['unit'=16,'feat'=8,'tm'=2] {'tm'}, dimensions={0}, use_global_device_ids=true | all-gather | bytes 49152 | tf_op jit(solution)/shard_map/all_gather | solution.py:16
  66.7 0.1 copy.10
  66.8 6.1 %multiply_reduce_fusion = (f32[64,16]{0,1:T(8,128)S(1)}, bf16[16,1024,64]{1,2,0:T(8,128)(2,1)S(1)}) fusion(f32[64,1024]{1,0:T(8,128)S(1)} %copy.26, bf16[16,1024,256]{2,1,0:T(8,128)(2,1)} %param.4, bf16[256,64]{0,1:T(8,128)(2,1)S(1)} %all_gather.6), kind=kOutput, calls=%fused_computation | convolution fusion | flops 540015616 | bytes 10784768 | tf_op jit(solution)/shard_map/jik,kr->jir/dot_general | solution.py:17
  72.9 0.0 copy-start.2
  72.9 1.3 fusion
  74.3 1.0 copy.25
  75.3 0.0 reduce-scatter.4.cloned.1.call-update
  75.3 0.0 copy-done.1
  75.3 0.2 fusion.16
  75.5 0.2 fusion.15
  75.7 0.0 copy-done.2
  75.7 0.2 fusion.14
  76.0 280.0 %psum.38 = f32[16,64]{1,0:T(8,128)S(1)} all-reduce(f32[16,64]{1,0:T(8,128)S(1)} %bitcast.57), channel_id=1, replica_groups=mesh['unit'=16,'feat'=8,'tm'=2] {'unit','feat'}, use_global_device_ids=true, to_apply=%region_4.0 | all-reduce | flops 1024 | bytes 8192 | tf_op jit(solution)/shard_map/psum | solution.py:30
  356.0 73.3 %psum.37 = f32[64,64]{1,0:T(8,128)S(1)} all-reduce(f32[64,64]{1,0:T(8,128)S(1)} %fusion.16), channel_id=1, replica_groups=mesh['unit'=16,'feat'=8,'tm'=2] {'unit','feat','tm'}, use_global_device_ids=true, to_apply=%region_3.0 | all-reduce | flops 4096 | bytes 32768 | tf_op jit(solution)/shard_map/psum | solution.py:44
  429.3 10.4 %psum.35 = f32[64,64]{1,0:T(8,128)S(1)} all-reduce(f32[64,64]{1,0:T(8,128)S(1)} %fusion.14), channel_id=1, replica_groups=mesh['unit'=16,'feat'=8,'tm'=2] {'tm'}, use_global_device_ids=true, to_apply=%region_0.0 | all-reduce | flops 4096 | bytes 32768 | tf_op jit(solution)/shard_map/psum | solution.py:45
  439.7 73.6 %psum.36 = f32[64,64]{1,0:T(8,128)S(1)} all-reduce(f32[64,64]{1,0:T(8,128)S(1)} %fusion.15), channel_id=1, replica_groups=mesh['unit'=16,'feat'=8,'tm'=2] {'feat','tm'}, use_global_device_ids=true, to_apply=%region_1.0 | all-reduce | flops 4096 | bytes 32768 | tf_op jit(solution)/shard_map/psum | solution.py:46
  513.3 0.7 fusion.7
  514.1 1.6 fusion.3
  515.7 0.8 copy.24
  516.5 0.2 fusion.5
  516.8 0.7 copy.8
  (5 shorter events, 0.0 us)
Async XLA Ops:
  8.0 506.1 %all-reduce.2.cloned.1.call-start = ((), (), s32[]{:S(2)}) async-start(), calls=%async_computation.1 | async-start | bytes 131072 | tf_op jit(solution)/shard_map/psum | solution.py:33
  53.9 6.8 %copy-start = (f32[128,64]{0,1:T(8,128)S(1)}, f32[128,64]{0,1:T(8,128)}, u32[]{:S(2)}) copy-start(f32[128,64]{0,1:T(8,128)} %param.7) | copy-start | bytes 98308
  60.4 455.2 %reduce-scatter.4.cloned.1.call-start = ((), (), s32[]{:S(2)}) async-start(), calls=%async_computation.2 | async-start | bytes 557056
  72.9 2.4 copy-start.1
  72.9 2.8 copy-start.2
Sparse Core Ops, SparseCore 0:
  60.6 102.2 all-reduce.1
Sparse Core Ops, SparseCore 1:
  75.4 197.1 reduce-scatter.3
where the time goes:
time: 525 us
  blocking collectives  488 us (93%)
  matrix products  16.5 us (3%)
  between operations  15.6 us (3%)
    psum x1, blocking collectives, body(): by_window = lax.psum(window_part, ('unit', 'feat'))  280 us
    psum x1, blocking collectives, body(): gram_feat = lax.psum(feat_gram_part, ('feat', 'tm'))  73.6 us
    psum x1, blocking collectives, body(): gram_unit = lax.psum(unit_gram_part, ('unit', 'feat', 'tm'))  73.3 us
    all_gather x1, blocking collectives, body(): lax.all_gather(unit_factor.astype(jnp.bfloat16), ('feat', 'tm'), axis=0,...  44.4 us
  transfers between devices with their start and end apart: 2, of which 0 were waited for; matrix products, arithmetic and copies ran while one was open for 2% of the time, Pallas kernels for 0%

commit v1 on v0

v1 whole, which is shorter than its diff:
```python
import functools
import math

import jax
import jax.numpy as jnp
from jax import lax
from jax.experimental import pallas as pl
from jax.experimental.pallas import tpu as pltpu
from jax.sharding import PartitionSpec as P

F32 = jnp.float32
BF16 = jnp.bfloat16
HIGH = lax.Precision.HIGHEST
NT = (((1,), (1,)), ((), ()))
TN = (((0,), (0,)), ((), ()))
GROUP = ("feat", "tm")
VMEM = pl.BlockSpec(memory_space=pltpu.VMEM)
HBM = pl.BlockSpec(memory_space=pltpu.HBM)


def call(kernel, out_shape, *args, name, far=(), **more):
    args = [
        pltpu.with_memory_space_constraint(arg, pltpu.HBM) if at in far else arg
        for at, arg in enumerate(args)
    ]
    return pl.pallas_call(
        kernel,
        out_shape=out_shape,
        in_specs=[HBM if at in far else VMEM for at in range(len(args))],
        out_specs=jax.tree.map(lambda _: VMEM, out_shape),
        compiler_params=pltpu.CompilerParams(vmem_limit_bytes=16 * 2**20),
        name=name,
        **more,
    )(*args)


def spread(rows):
    half = rows.shape[0] // 2
    return jnp.concatenate([rows[:half], rows[half:]], axis=-1)


def stack(rows):
    return jnp.concatenate([rows[:, :64], rows[:, 64:]], axis=0)


def low(value):
    return value.astype(BF16).astype(F32)


def split(value, axis):
    high_part = low(value)
    return jnp.concatenate([high_part, low(value - high_part)], axis=axis)


def dot(one, two):
    return jnp.dot(one, two, precision=HIGH, preferred_element_type=F32)


def prepare_kernel(
    unit_far, feat_far, window_far, gather_ref, pair_ref, feat_ref, window_ref, unit_ref, sems
):
    copies = [
        pltpu.make_async_copy(unit_far, unit_ref, sems.at[0]),
        pltpu.make_async_copy(feat_far, feat_ref, sems.at[1]),
        pltpu.make_async_copy(window_far, window_ref, sems.at[2]),
    ]
    for copy in copies:
        copy.start()
    copies[1].wait()
    copies[2].wait()
    parts = [split(feat_ref[...], 0), split(window_ref[...], -1)]
    pair_ref[...] = jnp.concatenate(parts, axis=0).astype(BF16)
    copies[0].wait()
    chunk = spread(unit_ref[...].T).astype(BF16)
    for at in range(16):
        gather_ref[at] = chunk


def fetches(tensor_far, places, sems, halved):
    rows = tensor_far.shape[1] // 2
    result, at = [], 0
    for window, place in places:
        parts = 2 if len(result) < halved else 1
        copies = []
        for part in range(parts):
            span = pl.ds(part * rows, rows * 2 // parts)
            source, target = tensor_far.at[window, span], place.at[span]
            copies.append(pltpu.make_async_copy(source, target, sems.at[at]))
            at += 1
        result.append(copies)
    for copies in result:
        for copy in copies:
            copy.start()
    return result


def unit_kernel(
    tensor_far, pair_ref, feat_ref, window_ref,
    kept_ref, out_ref, both_ref, gram_ref, tensor_ref, total, sems,
):
    windows, kept = tensor_far.shape[0], kept_ref.shape[0]
    places = [
        (j, kept_ref.at[j] if j < kept else tensor_ref.at[j - kept]) for j in range(windows)
    ]
    copies = fetches(tensor_far, places, sems, windows // 2)
    pair = pair_ref[0:128].astype(F32)
    mine, other = feat_ref[...], pair[0:64] + pair[64:128]
    first = lax.axis_index("tm") == 0
    feat = jnp.concatenate(
        [jnp.where(first, mine, other), jnp.where(first, other, mine)], axis=-1
    )
    gram = lax.dot_general(feat, feat, NT, precision=HIGH, preferred_element_type=F32)
    place = lax.broadcasted_iota(jnp.int32, (64, 64), 0) // 16 == lax.axis_index("unit") // 4
    gram = jnp.sum(jnp.where(place, gram, 0.0).reshape(4, 16, 64), axis=0)
    gram_ref[...] = split(gram, -1).astype(BF16)
    both_ref[...] = low(feat)
    feat = feat.astype(BF16)
    window = low(window_ref[...]).T
    for j in range(windows):
        for copy in copies[j]:
            copy.wait()
        part = lax.dot_general(feat, places[j][1][...], NT, preferred_element_type=F32)
        part = part * window[:, j : j + 1]
        if j == 0:
            total[...] = part
        else:
            total[...] += part
    left = lax.broadcasted_iota(jnp.int32, (32, 128), 1) < 64
    for at in range(0, 16, 2):
        top = total[0:32, at * 64 : at * 64 + 128]
        bottom = total[32:64, at * 64 : at * 64 + 128]
        out_ref[at] = jnp.where(left, top, pltpu.roll(bottom, 64, 1)).astype(BF16)
        out_ref[at + 1] = jnp.where(left, pltpu.roll(top, 64, 1), bottom).astype(BF16)


def feature_kernel(
    tensor_far, kept_ref, gather_ref, both_ref, window_ref,
    sums_ref, tensor_ref, unit_ref, total, products, sems,
):
    windows, kept = tensor_far.shape[0], kept_ref.shape[0]
    places = [(j, tensor_ref.at[j - kept]) for j in range(kept, windows)]
    copies = fetches(tensor_far, places, sems, (windows - kept) // 2)
    left = lax.broadcasted_iota(jnp.int32, (32, 128), 1) < 64
    for at in range(0, 16, 2):
        one = gather_ref[at].astype(F32)
        two = gather_ref[at + 1].astype(F32)
        columns = pl.ds(at * 64, 128)
        unit_ref[0:32, columns] = jnp.where(left, one, pltpu.roll(two, 64, 1)).astype(BF16)
        unit_ref[32:64, columns] = jnp.where(left, pltpu.roll(one, 64, 1), two).astype(BF16)
    unit = unit_ref[...]
    feat = both_ref[...]
    window = low(window_ref[...]).T
    for j in range(windows):
        if j < kept:
            slab = kept_ref[j]
        else:
            for copy in copies[j - kept]:
                copy.wait()
            slab = tensor_ref[j - kept]
        second = jnp.dot(unit, slab, preferred_element_type=F32)
        product = second * feat
        products[j] = product[:, :128] + product[:, 128:]
        second = second * window[:, j : j + 1]
        if j == 0:
            total[...] = second
        else:
            total[...] += second
    gram = lax.dot_general(unit, unit, NT, preferred_element_type=F32)
    rest = jnp.concatenate([spread(gram), spread(jnp.sum(products[...], axis=-1))], axis=0)
    parts = [total[:, :128], total[:, 128:], split(rest, 0)]
    sums_ref[...] = jnp.concatenate(parts, axis=0).astype(BF16)


def add_four(refs):
    one, two, three, four = [ref[...].astype(F32) for ref in refs]
    return (one + two) + (three + four)


def near_kernel(s0, s1, s2, s3, by_unit_ref, gram_ref, scatter_ref, send_ref, keep_ref):
    total = add_four((s0, s1, s2, s3))
    rest = total[128:168] + total[168:208]
    tm = lax.axis_index("tm")
    first = tm == 0
    send_ref[...] = jnp.where(first, total[64:128], total[0:64])
    keep_ref[0:64] = jnp.where(first, total[0:64], total[64:128])
    keep_ref[64:96] = rest[0:32]
    by_window = split(rest[32:40], 0)
    gram = gram_ref[...].astype(F32)
    for at in range(16):
        scatter_ref[at, 0:32] = by_unit_ref[at]
        scatter_ref[at, 32:48] = jnp.where(tm == at % 2, by_window, gram).astype(BF16)


def group_kernel(scatter_ref, keep_ref, other_ref, unit_ref, sums_ref):
    even = scatter_ref[0].astype(F32)
    odd = scatter_ref[1].astype(F32)
    for at in range(2, 16, 2):
        even += scatter_ref[at].astype(F32)
        odd += scatter_ref[at + 1].astype(F32)
    unit_ref[...] = even[0:32] + odd[0:32]
    first = lax.axis_index("tm") == 0
    by_window = jnp.where(first, even[32:48], odd[32:48])
    gram = jnp.where(first, odd[32:48], even[32:48])
    gram = jnp.concatenate([gram[:, :64] + gram[:, 64:]] * 4, axis=0)
    place = lax.broadcasted_iota(jnp.int32, (64, 64), 0) // 16 == lax.axis_index("unit") // 4
    sums_ref[0:64] = keep_ref[0:64] + other_ref[...]
    sums_ref[64:96] = keep_ref[64:96]
    sums_ref[96:128] = spread(jnp.where(place, gram, 0.0))
    sums_ref[128:136] = by_window[0:8] + by_window[8:16]


def gradient_kernel(
    scales, s0, s1, s2, s3, by_unit_ref, unit_ref, window_ref, feat_ref, pair_ref,
    grad_unit_ref, grad_window_ref, grad_feat_ref,
):
    total = add_four((s0, s1, s2, s3))
    gram_unit, gram_feat = stack(total[64:96]), stack(total[96:128])
    window = window_ref[...]
    other = pair_ref[128:144, :].astype(F32)
    other = other[:, :64] + other[:, 64:]
    windows = jnp.concatenate([window, other], axis=0)
    gram_window = lax.dot_general(
        windows, windows, TN, precision=HIGH, preferred_element_type=F32
    )
    grad_unit_ref[...] = (
        dot(unit_ref[...], gram_window * gram_feat) - stack(by_unit_ref[...]).T
    ) * scales[0]
    grad_window_ref[...] = (
        dot(window, gram_unit * gram_feat) - stack(total[128:136])
    ) * scales[1]
    grad_feat_ref[...] = (dot(gram_unit * gram_window, feat_ref[...]) - total[0:64]) * scales[2]


def by_xor(value, mask):
    count = lax.axis_size("unit")
    return lax.ppermute(value, "unit", [(i, i ^ mask) for i in range(count)])


def body(tensor, unit_factor, window_factor, feat_factor):
    win_rows, unit_count, feat_count = tensor.shape
    units_all = unit_count * lax.axis_size("unit")
    windows_all = win_rows * lax.axis_size("tm")
    feats_all = feat_count * lax.axis_size("feat")
    shape = jax.ShapeDtypeStruct
    feat = feat_factor.T
    gather, pair, feat_near, window_near = call(
        prepare_kernel,
        [
            shape((16, 32, 128), BF16),
            shape((144, 128), BF16),
            shape((64, 128), F32),
            shape((win_rows, 64), F32),
        ],
        unit_factor, feat, window_factor,
        far=(0, 1, 2),
        scratch_shapes=[pltpu.VMEM((64, 64), F32), pltpu.SemaphoreType.DMA((3,))],
        name="prepare",
    )
    pair = lax.ppermute(pair, "tm", [(0, 1), (1, 0)])
    gather = lax.all_to_all(gather.reshape(512, 128), GROUP, 0, 0, tiled=True).reshape(16, 32, 128)
    cost = pl.CostEstimate(flops=2**33, bytes_accessed=2**23, transcendentals=0)
    kept = 6
    kept_windows, by_unit, both, gram = call(
        unit_kernel,
        [
            pltpu.VMEM((kept, unit_count, feat_count), BF16),
            shape((16, 32, 128), BF16),
            shape((64, feat_count), F32),
            shape((16, 128), BF16),
        ],
        tensor, pair, feat_near, window_near,
        far=(0,),
        scratch_shapes=[
            pltpu.VMEM((win_rows - kept, unit_count, feat_count), BF16),
            pltpu.VMEM((64, unit_count), F32),
            pltpu.SemaphoreType.DMA((2 * win_rows,)),
        ],
        cost_estimate=cost,
        name="by_unit",
    )
    sums = call(
        feature_kernel,
        shape((208, 128), BF16),
        tensor, pltpu.with_memory_space_constraint(kept_windows, pltpu.VMEM), gather, both, window_near,
        far=(0,),
        scratch_shapes=[
            pltpu.VMEM((win_rows - kept, unit_count, feat_count), BF16),
            pltpu.VMEM((64, unit_count), BF16),
            pltpu.VMEM((64, feat_count), F32),
            pltpu.VMEM((win_rows, 64, 128), F32),
            pltpu.SemaphoreType.DMA((2 * win_rows,)),
        ],
        cost_estimate=cost,
        name="by_feature",
    )
    near = [by_xor(sums, mask) for mask in (1, 2, 3)]
    scatter, send, keep = call(
        near_kernel,
        [shape((16, 48, 128), BF16), shape((64, 128), F32), shape((96, 128), F32)],
        sums, *near, by_unit, gram,
        name="near_sums",
    )
    other = lax.ppermute(send, "tm", [(0, 1), (1, 0)])
    scatter = lax.all_to_all(scatter.reshape(768, 128), GROUP, 0, 0, tiled=True).reshape(16, 48, 128)
    by_unit, sums = call(
        group_kernel,
        [shape((32, 128), F32), shape((136, 128), F32)],
        scatter, keep, other,
        name="group_sums",
    )
    far = [by_xor(sums, mask) for mask in (8, 4, 12)]
    scales = (
        1 / math.sqrt(windows_all * feats_all),
        1 / math.sqrt(units_all * feats_all),
        1 / math.sqrt(units_all * windows_all),
    )
    grad_unit, grad_window, grad_feat = call(
        functools.partial(gradient_kernel, scales),
        [shape((64, 64), F32), shape((win_rows, 64), F32), shape((64, 128), F32)],
        sums, *far, by_unit, unit_factor, window_factor, feat, pair,
        name="gradients",
    )
    return grad_unit, grad_window, grad_feat.T


def solution(mesh):
    in_specs = (
        P("tm", "unit", "feat"),
        P(("unit", "feat", "tm"), None),
        P("tm", None),
        P(("feat", "tm"), None),
    )
    out_specs = (P(("unit", "feat", "tm"), None), P("tm", None), P(("feat", "tm"), None))
    return jax.shard_map(body, mesh=mesh, in_specs=in_specs, out_specs=out_specs, check_vma=False)
```

time: 525 us -> 67 us (0.13)
  blocking collectives: 488 us -> 0 us
  starting transfers between devices: 0.08 us -> 28.2 us
  waiting for transfers between devices: 0.04 us -> 19.7 us
  matrix products: 16.5 us -> 0 us
  between operations: 15.6 us -> 0.72 us
  Pallas kernels: 0 us -> 14.5 us
    psum x4 -> x0, blocking collectives: 437 us -> none  [the longest x1 280 us: body(): by_window = lax.psum(window_part, ('unit', 'feat'))]
    all_gather x2 -> x0, blocking collectives: 50.3 us -> none  [the longest x1 44.4 us: body(): lax.all_gather(unit_factor.astype(jnp.bfloat16), ('feat', 'tm'), axis=0,...]
    dot_general x9 -> x0, matrix products: 16.5 us -> none  [the longest x1 6.13 us: body(): jnp.einsum('jik,kr->jir', tensor, feat_low, preferred_element_type=jnp.fl...]
    all_to_all x0 -> x2, starting transfers between devices: none -> 15.6 us  [the longest x1 9.41 us: body(): lax.all_to_all(gather.reshape(512, 128), GROUP, 0, 0, tiled=True)]
    pallas_call x0 -> x6, Pallas kernels: none -> 14.5 us  [call(): pl.pallas_call(kernel, out_shape=out_shape, in_specs=[HBM if at in far el...]
    ppermute x0 -> x8, starting transfers between devices: none -> 12.6 us  [the longest x6 6.94 us: by_xor(): return lax.ppermute(value, 'unit', [(i, i ^ mask) for i in range(count)])]
    all_to_all x0 -> x2, waiting for transfers between devices: none -> 10.4 us  [the longest x1 6.95 us: body(): lax.all_to_all(scatter.reshape(768, 128), GROUP, 0, 0, tiled=True)]
    ppermute x0 -> x8, waiting for transfers between devices: none -> 9.37 us  [the longest x6 7.14 us: by_xor(): return lax.ppermute(value, 'unit', [(i, i ^ mask) for i in range(count)])]
  transfers between devices with their start and end apart: 2 -> 10, of which waited for: 0 -> 7; matrix products, arithmetic and copies ran while one was open for 2% -> 0% of each run, Pallas kernels for 0% -> 9%
where the time goes in v1:
time: 67 us; the launch traced here: 66.7 us
  starting transfers between devices  28.2 us (42%)
  waiting for transfers between devices  19.7 us (29%)
  Pallas kernels  14.5 us (22%)
  local copies, waits for them, and re-layouts  3.54 us (5%)
  between operations  0.72 us (1%)
    pallas_call x6, Pallas kernels, call(): pl.pallas_call(kernel, out_shape=out_shape, in_specs=[HBM if at in far el...  14.5 us
    all_to_all x1, starting transfers between devices, body(): lax.all_to_all(gather.reshape(512, 128), GROUP, 0, 0, tiled=True)  9.41 us
    ppermute x6, waiting for transfers between devices, by_xor(): return lax.ppermute(value, 'unit', [(i, i ^ mask) for i in range(count)])  7.14 us
    all_to_all x1, waiting for transfers between devices, body(): lax.all_to_all(scatter.reshape(768, 128), GROUP, 0, 0, tiled=True)  6.95 us
    ppermute x6, starting transfers between devices, by_xor(): return lax.ppermute(value, 'unit', [(i, i ^ mask) for i in range(count)])  6.94 us
    all_to_all x1, starting transfers between devices, body(): lax.all_to_all(scatter.reshape(768, 128), GROUP, 0, 0, tiled=True)  6.19 us
    unnamed x10, local copies, waits for them, and re-layouts  3.54 us
    ppermute x1, starting transfers between devices, body(): other = lax.ppermute(send, 'tm', [(0, 1), (1, 0)])  3.43 us
  transfers between devices with their start and end apart: 10, of which 7 were waited for; matrix products, arithmetic and copies ran while one was open for 0% of the time, Pallas kernels for 9%

profile of v1, /device:TPU:2, one launch (start us, length us, event | category | flops | bytes accessed | tf_op | source)
XLA Modules:
  0.0 66.7 jit_solution(1588379926199341914)
XLA Ops:
  0.6 1.7 %prepare.1 = (bf16[16,32,128]{2,1,0:T(8,128)(2,1)}, bf16[144,128]{1,0:T(8,128)(2,1)S(1)}, f32[64,128]{1,0:T(8,128)S(1)}, f32[16,64]{1,0:T(8,128)S(1)}) custom-call(f32[64,64]{1,0:T(8,128)} %unit_ref.1, f32[64,128]{1,0:T(8,128)} %bitcast.2, f32[16,64]{1,0:T(8,128)} %window_ref.1), custom_call_target="tpu_custom_call" | custom-call | tf_op jit(solution)/shard_map/prepare/pallas_call | solution.py:26
  2.3 2.2 %collective-permute-start = (bf16[144,128]{1,0:T(8,128)(2,1)S(1)}, bf16[144,128]{1,0:T(8,128)(2,1)S(1)}, u32[]{:S(2)}, u32[]{:S(2)}) collective-permute-start(bf16[144,128]{1,0:T(8,128)(2,1)S(1)} %get-tuple-element.19), channel_id=1, source_target_pairs={{0,1},{1,0},{2,3},{3,2},{4,5},{5,4},{6,7},{7,6},{8,9},{9,8},{10,11... | collective-permute-start | bytes 110600 | tf_op jit(solution)/shard_map/ppermute | solution.py:259
  4.5 9.4 %all-to-all-start = ((bf16[16,32,128]{2,1,0:T(8,128)(2,1)}), bf16[16,32,128]{2,1,0:T(8,128)(2,1)S(1)}, u32[]{:S(2)}, u32[]{:S(2)}) async-start(bf16[16,32,128]{2,1,0:T(8,128)(2,1)} %get-tuple-element.23), calls=%async_computation | async-start | bytes 262144 | tf_op jit(solution)/shard_map/all_to_all | solution.py:260
  13.9 0.0 collective-permute-done.pair_ref
  14.0 6.0 %by_unit.1 = (bf16[6,1024,256]{2,1,0:T(8,128)(2,1)S(1)}, bf16[16,32,128]{2,1,0:T(8,128)(2,1)S(1)}, f32[64,256]{1,0:T(8,128)S(1)}, bf16[16,128]{1,0:T(8,128)(2,1)S(1)}) custom-call(bf16[16,1024,256]{2,1,0:T(8,128)(2,1)} %tensor_far.3, bf16[144,128]{1,0:T(8,128)(2,1)S(1)} %collective-permute-done.pair_ref, f32[64,128]{1,0:T(8,128)S(1)} %get-tuple-element.20.feat_ref, ...), custom_call_target="tpu_custom_call" | custom-call | flops 8589934592 | bytes 8388608 | tf_op jit(solution)/shard_map/by_unit/pallas_call | solution.py:26
  20.0 0.0 copy-start.3
  20.0 1.6 %copy-done.3 = bf16[6,1024,256]{2,1,0:T(8,128)(2,1)} copy-done((bf16[6,1024,256]{2,1,0:T(8,128)(2,1)}, bf16[6,1024,256]{2,1,0:T(8,128)(2,1)S(1)}, u32[]{:S(2)}) %copy-start.3) | copy-done | bytes 3145752
  21.7 3.4 %all-to-all-done.gather_ref = bf16[16,32,128]{2,1,0:T(8,128)(2,1)S(1)} async-done(((bf16[16,32,128]{2,1,0:T(8,128)(2,1)}), bf16[16,32,128]{2,1,0:T(8,128)(2,1)S(1)}, u32[]{:S(2)}, u32[]{:S(2)}) %all-to-all-start) | async-done | bytes 131104 | tf_op jit(solution)/shard_map/all_to_all | solution.py:260
  25.1 1.9 %copy-done.4 = bf16[6,1024,256]{2,1,0:T(8,128)(2,1)S(1)} copy-done((bf16[6,1024,256]{2,1,0:T(8,128)(2,1)S(1)}, bf16[6,1024,256]{2,1,0:T(8,128)(2,1)}, u32[]{:S(2)}) %copy-start.4) | copy-done | bytes 3145752
  27.0 4.8 %by_feature.1.s0 = bf16[208,128]{1,0:T(8,128)(2,1)S(1)} custom-call(bf16[16,1024,256]{2,1,0:T(8,128)(2,1)} %tensor_far.3, bf16[6,1024,256]{2,1,0:T(8,128)(2,1)S(1)} %copy-done.4, bf16[16,32,128]{2,1,0:T(8,128)(2,1)S(1)} %all-to-all-done.gather_ref, f32[64,256]{1,0:T(8,128)S(1)} %get-tuple-element.24.both_ref, f32[16,64]{1,0:T(8,128)S(1)} %get-tuple-element.21.window_ref), custom_call_target="tpu_custom_call" | custom-call | flops 8589934592 | bytes 8388608 | tf_op jit(solution)/shard_map/by_feature/pallas_call | solution.py:26
  31.7 0.1 collective-permute-start.3
  31.8 1.7 %collective-permute-start.2 = (bf16[208,128]{1,0:T(8,128)(2,1)S(1)}, bf16[208,128]{1,0:T(8,128)(2,1)S(1)}, u32[]{:S(2)}, u32[]{:S(2)}) collective-permute-start(bf16[208,128]{1,0:T(8,128)(2,1)S(1)} %by_feature.1.s0), channel_id=1, source_target_pairs={{0,32},{16,48},{32,0},{48,16},{64,96},{80,112},{96,64},{112,80},{1... | collective-permute-start | bytes 159752 | tf_op jit(solution)/shard_map/ppermute | solution.py:236
  33.5 0.2 collective-permute-start.1
  33.7 2.1 %collective-permute-done.3.s3 = bf16[208,128]{1,0:T(8,128)(2,1)S(1)} collective-permute-done((bf16[208,128]{1,0:T(8,128)(2,1)S(1)}, bf16[208,128]{1,0:T(8,128)(2,1)S(1)}, u32[]{:S(2)}, u32[]{:S(2)}) %collective-permute-start.3) | collective-permute-done | bytes 53280 | tf_op jit(solution)/shard_map/ppermute | solution.py:236
  35.8 1.1 %collective-permute-done.2.s2 = bf16[208,128]{1,0:T(8,128)(2,1)S(1)} collective-permute-done((bf16[208,128]{1,0:T(8,128)(2,1)S(1)}, bf16[208,128]{1,0:T(8,128)(2,1)S(1)}, u32[]{:S(2)}, u32[]{:S(2)}) %collective-permute-start.2) | collective-permute-done | bytes 53280 | tf_op jit(solution)/shard_map/ppermute | solution.py:236
  36.9 0.0 collective-permute-done.1.s1
  36.9 0.7 %near_sums.1 = (bf16[16,48,128]{2,1,0:T(8,128)(2,1)}, f32[64,128]{1,0:T(8,128)S(1)}, f32[96,128]{1,0:T(8,128)S(1)}) custom-call(bf16[208,128]{1,0:T(8,128)(2,1)S(1)} %by_feature.1.s0, bf16[208,128]{1,0:T(8,128)(2,1)S(1)} %collective-permute-done.1.s1, bf16[208,128]{1,0:T(8,128)(2,1)S(1)} %collective-permute-done.2.s2, ...), custom_call_target="tpu_custom_call" | custom-call | tf_op jit(solution)/shard_map/near_sums/pallas_call | solution.py:26
  37.6 6.2 %all-to-all-start.1 = ((bf16[16,48,128]{2,1,0:T(8,128)(2,1)}), bf16[16,48,128]{2,1,0:T(8,128)(2,1)S(1)}, u32[]{:S(2)}, u32[]{:S(2)}) async-start(bf16[16,48,128]{2,1,0:T(8,128)(2,1)} %get-tuple-element.27), calls=%async_computation.1 | async-start | bytes 393216 | tf_op jit(solution)/shard_map/all_to_all | solution.py:304
  43.8 3.4 %collective-permute-start.4 = (f32[64,128]{1,0:T(8,128)S(1)}, f32[64,128]{1,0:T(8,128)S(1)}, u32[]{:S(2)}, u32[]{:S(2)}) collective-permute-start(f32[64,128]{1,0:T(8,128)S(1)} %get-tuple-element.29), channel_id=1, source_target_pairs={{0,1},{1,0},{2,3},{3,2},{4,5},{5,4},{6,7},{7,6},{8,9},{9,8},{10,11... | collective-permute-start | bytes 98312 | tf_op jit(solution)/shard_map/ppermute | solution.py:303
  47.2 2.2 %collective-permute-done.4.other_ref = f32[64,128]{1,0:T(8,128)S(1)} collective-permute-done((f32[64,128]{1,0:T(8,128)S(1)}, f32[64,128]{1,0:T(8,128)S(1)}, u32[]{:S(2)}, u32[]{:S(2)}) %collective-permute-start.4) | collective-permute-done | bytes 32800 | tf_op jit(solution)/shard_map/ppermute | solution.py:303
  49.5 6.9 %all-to-all-done.1.scatter_ref = bf16[16,48,128]{2,1,0:T(8,128)(2,1)S(1)} async-done(((bf16[16,48,128]{2,1,0:T(8,128)(2,1)}), bf16[16,48,128]{2,1,0:T(8,128)(2,1)S(1)}, u32[]{:S(2)}, u32[]{:S(2)}) %all-to-all-start.1) | async-done | bytes 196640 | tf_op jit(solution)/shard_map/all_to_all | solution.py:304
  56.4 0.2 group_sums.1
  56.6 3.1 %collective-permute-start.7 = (f32[136,128]{1,0:T(8,128)S(1)}, f32[136,128]{1,0:T(8,128)S(1)}, u32[]{:S(2)}, u32[]{:S(2)}) collective-permute-start(f32[136,128]{1,0:T(8,128)S(1)} %get-tuple-element.30.s0), channel_id=1, source_target_pairs={{0,192},{16,208},{32,224},{48,240},{64,128},{80,144},{96,160},{112... | collective-permute-start | bytes 208904 | tf_op jit(solution)/shard_map/ppermute | solution.py:236
  59.7 0.5 collective-permute-start.6
  60.2 1.4 %collective-permute-start.5 = (f32[136,128]{1,0:T(8,128)S(1)}, f32[136,128]{1,0:T(8,128)S(1)}, u32[]{:S(2)}, u32[]{:S(2)}) collective-permute-start(f32[136,128]{1,0:T(8,128)S(1)} %get-tuple-element.30.s0), channel_id=1, source_target_pairs={{0,128},{16,144},{32,160},{48,176},{64,192},{80,208},{96,224},{112... | collective-permute-start | bytes 208904 | tf_op jit(solution)/shard_map/ppermute | solution.py:236
  61.6 2.1 %collective-permute-done.7.s3 = f32[136,128]{1,0:T(8,128)S(1)} collective-permute-done((f32[136,128]{1,0:T(8,128)S(1)}, f32[136,128]{1,0:T(8,128)S(1)}, u32[]{:S(2)}, u32[]{:S(2)}) %collective-permute-start.7) | collective-permute-done | bytes 69664 | tf_op jit(solution)/shard_map/ppermute | solution.py:236
  63.7 1.8 %collective-permute-done.6.s2 = f32[136,128]{1,0:T(8,128)S(1)} collective-permute-done((f32[136,128]{1,0:T(8,128)S(1)}, f32[136,128]{1,0:T(8,128)S(1)}, u32[]{:S(2)}, u32[]{:S(2)}) %collective-permute-start.6) | collective-permute-done | bytes 69664 | tf_op jit(solution)/shard_map/ppermute | solution.py:236
  65.5 0.0 collective-permute-done.5.s1
  65.5 0.0 copy-done
  65.5 0.0 copy-done.1
  65.5 0.0 copy-done.2
  65.5 1.2 %gradients.1 = (f32[64,64]{1,0:T(8,128)}, f32[16,64]{1,0:T(8,128)}, f32[64,128]{1,0:T(8,128)}) custom-call(f32[136,128]{1,0:T(8,128)S(1)} %get-tuple-element.30.s0, f32[136,128]{1,0:T(8,128)S(1)} %collective-permute-done.5.s1, f32[136,128]{1,0:T(8,128)S(1)} %collective-permute-done.6.s2, f32[136,128]{1,0:T(8,128)S(1)} %collective-permute-done.7.s3, ...), custom_call_target="tpu_custom_call" | custom-call | tf_op jit(solution)/shard_map/gradients/pallas_call | solution.py:26
  (4 shorter events, 0.0 us)
Async XLA Ops:
  2.3 11.6 %collective-permute-start = (bf16[144,128]{1,0:T(8,128)(2,1)S(1)}, bf16[144,128]{1,0:T(8,128)(2,1)S(1)}, u32[]{:S(2)}, u32[]{:S(2)}) collective-permute-start(bf16[144,128]{1,0:T(8,128)(2,1)S(1)} %get-tuple-element.19), channel_id=1, source_target_pairs={{0,1},{1,0},{2,3},{3,2},{4,5},{5,4},{6,7},{7,6},{8,9},{9,8},{10,11... | collective-permute-start | bytes 110600 | tf_op jit(solution)/shard_map/ppermute | solution.py:259
  4.5 20.5 %all-to-all-start = ((bf16[16,32,128]{2,1,0:T(8,128)(2,1)}), bf16[16,32,128]{2,1,0:T(8,128)(2,1)S(1)}, u32[]{:S(2)}, u32[]{:S(2)}) async-start(bf16[16,32,128]{2,1,0:T(8,128)(2,1)} %get-tuple-element.23), calls=%async_computation | async-start | bytes 262144 | tf_op jit(solution)/shard_map/all_to_all | solution.py:260
  20.0 1.7 %copy-start.3 = (bf16[6,1024,256]{2,1,0:T(8,128)(2,1)}, bf16[6,1024,256]{2,1,0:T(8,128)(2,1)S(1)}, u32[]{:S(2)}) copy-start(bf16[6,1024,256]{2,1,0:T(8,128)(2,1)S(1)} %get-tuple-element.22.kept_ref) | copy-start | bytes 9437188
  25.1 1.9 %copy-start.4 = (bf16[6,1024,256]{2,1,0:T(8,128)(2,1)S(1)}, bf16[6,1024,256]{2,1,0:T(8,128)(2,1)}, u32[]{:S(2)}) copy-start(bf16[6,1024,256]{2,1,0:T(8,128)(2,1)} %copy-done.3) | copy-start | bytes 9437188
  27.0 38.5 %copy-start = (f32[64,64]{1,0:T(8,128)S(1)}, f32[64,64]{1,0:T(8,128)}, u32[]{:S(2)}) copy-start(f32[64,64]{1,0:T(8,128)} %unit_ref.1) | copy-start | bytes 49156
  27.0 38.5 %copy-start.1 = (f32[128,64]{0,1:T(8,128)S(1)}, f32[128,64]{0,1:T(8,128)}, u32[]{:S(2)}) copy-start(f32[128,64]{0,1:T(8,128)} %param.7) | copy-start | bytes 98308
  27.0 38.5 %copy-start.2 = (f32[16,64]{1,0:T(8,128)S(1)}, f32[16,64]{1,0:T(8,128)}, u32[]{:S(2)}) copy-start(f32[16,64]{1,0:T(8,128)} %window_ref.1) | copy-start | bytes 12292
  31.7 4.1 %collective-permute-start.3 = (bf16[208,128]{1,0:T(8,128)(2,1)S(1)}, bf16[208,128]{1,0:T(8,128)(2,1)S(1)}, u32[]{:S(2)}, u32[]{:S(2)}) collective-permute-start(bf16[208,128]{1,0:T(8,128)(2,1)S(1)} %by_feature.1.s0), channel_id=1, source_target_pairs={{0,48},{16,32},{32,16},{48,0},{64,112},{80,96},{96,80},{112,64},{1... | collective-permute-start | bytes 159752 | tf_op jit(solution)/shard_map/ppermute | solution.py:236
  31.8 5.1 %collective-permute-start.2 = (bf16[208,128]{1,0:T(8,128)(2,1)S(1)}, bf16[208,128]{1,0:T(8,128)(2,1)S(1)}, u32[]{:S(2)}, u32[]{:S(2)}) collective-permute-start(bf16[208,128]{1,0:T(8,128)(2,1)S(1)} %by_feature.1.s0), channel_id=1, source_target_pairs={{0,32},{16,48},{32,0},{48,16},{64,96},{80,112},{96,64},{112,80},{1... | collective-permute-start | bytes 159752 | tf_op jit(solution)/shard_map/ppermute | solution.py:236
  33.5 3.4 %collective-permute-start.1 = (bf16[208,128]{1,0:T(8,128)(2,1)S(1)}, bf16[208,128]{1,0:T(8,128)(2,1)S(1)}, u32[]{:S(2)}, u32[]{:S(2)}) collective-permute-start(bf16[208,128]{1,0:T(8,128)(2,1)S(1)} %by_feature.1.s0), channel_id=1, source_target_pairs={{0,16},{16,0},{32,48},{48,32},{64,80},{80,64},{96,112},{112,96},{1... | collective-permute-start | bytes 159752 | tf_op jit(solution)/shard_map/ppermute | solution.py:236
  37.6 18.8 %all-to-all-start.1 = ((bf16[16,48,128]{2,1,0:T(8,128)(2,1)}), bf16[16,48,128]{2,1,0:T(8,128)(2,1)S(1)}, u32[]{:S(2)}, u32[]{:S(2)}) async-start(bf16[16,48,128]{2,1,0:T(8,128)(2,1)} %get-tuple-element.27), calls=%async_computation.1 | async-start | bytes 393216 | tf_op jit(solution)/shard_map/all_to_all | solution.py:304
  43.8 5.7 %collective-permute-start.4 = (f32[64,128]{1,0:T(8,128)S(1)}, f32[64,128]{1,0:T(8,128)S(1)}, u32[]{:S(2)}, u32[]{:S(2)}) collective-permute-start(f32[64,128]{1,0:T(8,128)S(1)} %get-tuple-element.29), channel_id=1, source_target_pairs={{0,1},{1,0},{2,3},{3,2},{4,5},{5,4},{6,7},{7,6},{8,9},{9,8},{10,11... | collective-permute-start | bytes 98312 | tf_op jit(solution)/shard_map/ppermute | solution.py:303
  56.6 7.1 %collective-permute-start.7 = (f32[136,128]{1,0:T(8,128)S(1)}, f32[136,128]{1,0:T(8,128)S(1)}, u32[]{:S(2)}, u32[]{:S(2)}) collective-permute-start(f32[136,128]{1,0:T(8,128)S(1)} %get-tuple-element.30.s0), channel_id=1, source_target_pairs={{0,192},{16,208},{32,224},{48,240},{64,128},{80,144},{96,160},{112... | collective-permute-start | bytes 208904 | tf_op jit(solution)/shard_map/ppermute | solution.py:236
  59.7 5.8 %collective-permute-start.6 = (f32[136,128]{1,0:T(8,128)S(1)}, f32[136,128]{1,0:T(8,128)S(1)}, u32[]{:S(2)}, u32[]{:S(2)}) collective-permute-start(f32[136,128]{1,0:T(8,128)S(1)} %get-tuple-element.30.s0), channel_id=1, source_target_pairs={{0,64},{16,80},{32,96},{48,112},{64,0},{80,16},{96,32},{112,48},{1... | collective-permute-start | bytes 208904 | tf_op jit(solution)/shard_map/ppermute | solution.py:236
  60.2 5.3 %collective-permute-start.5 = (f32[136,128]{1,0:T(8,128)S(1)}, f32[136,128]{1,0:T(8,128)S(1)}, u32[]{:S(2)}, u32[]{:S(2)}) collective-permute-start(f32[136,128]{1,0:T(8,128)S(1)} %get-tuple-element.30.s0), channel_id=1, source_target_pairs={{0,128},{16,144},{32,160},{48,176},{64,192},{80,208},{96,224},{112... | collective-permute-start | bytes 208904 | tf_op jit(solution)/shard_map/ppermute | solution.py:236

commit v2 on v1

v2 whole, which is shorter than its diff:
```python
import functools
import math

import jax
import jax.numpy as jnp
from jax import lax
from jax.experimental import pallas as pl
from jax.experimental.pallas import tpu as pltpu
from jax.sharding import PartitionSpec as P

F32 = jnp.float32
BF16 = jnp.bfloat16
HIGH = lax.Precision.HIGHEST
NT = (((1,), (1,)), ((), ()))
TN = (((0,), (0,)), ((), ()))
GROUP = ("feat", "tm")
VMEM = pl.BlockSpec(memory_space=pltpu.VMEM)
HBM = pl.BlockSpec(memory_space=pltpu.HBM)


def call(kernel, out_shape, *args, name, far=(), **more):
    args = [
        pltpu.with_memory_space_constraint(arg, pltpu.HBM) if at in far else arg
        for at, arg in enumerate(args)
    ]
    return pl.pallas_call(
        kernel,
        out_shape=out_shape,
        in_specs=[HBM if at in far else VMEM for at in range(len(args))],
        out_specs=jax.tree.map(lambda _: VMEM, out_shape),
        compiler_params=pltpu.CompilerParams(vmem_limit_bytes=16 * 2**20),
        name=name,
        **more,
    )(*args)


def spread(rows):
    half = rows.shape[0] // 2
    return jnp.concatenate([rows[:half], rows[half:]], axis=-1)


def stack(rows):
    return jnp.concatenate([rows[:, :64], rows[:, 64:]], axis=0)


def low(value):
    return value.astype(BF16).astype(F32)


def split(value, axis):
    high_part = low(value)
    return jnp.concatenate([high_part, low(value - high_part)], axis=axis)


def dot(one, two):
    return jnp.dot(one, two, precision=HIGH, preferred_element_type=F32)


def prepare_kernel(
    unit_far, feat_far, window_far, gather_ref, pair_ref, feat_ref, window_ref, unit_ref, sems
):
    copies = [
        pltpu.make_async_copy(unit_far, unit_ref, sems.at[0]),
        pltpu.make_async_copy(feat_far, feat_ref, sems.at[1]),
        pltpu.make_async_copy(window_far, window_ref, sems.at[2]),
    ]
    for copy in copies:
        copy.start()
    copies[1].wait()
    copies[2].wait()
    parts = [split(feat_ref[...], 0), split(window_ref[...], -1)]
    pair_ref[...] = jnp.concatenate(parts, axis=0).astype(BF16)
    copies[0].wait()
    chunk = spread(unit_ref[...].T).astype(BF16)
    for at in range(16):
        gather_ref[at] = chunk


def fetches(tensor_far, places, sems):
    rows = tensor_far.shape[1] // 2
    result = []
    for at, (window, place) in enumerate(places):
        copies = []
        for part in range(2):
            span = pl.ds(part * rows, rows)
            source, target = tensor_far.at[window, span], place.at[span]
            copies.append(pltpu.make_async_copy(source, target, sems.at[2 * at + part]))
        result.append(copies)
    return result


def start(batch):
    for copies in batch:
        for copy in copies:
            copy.start()


def add_to(total, part, fresh):
    if fresh:
        total[...] = part
    else:
        total[...] += part


def by_unit_part(feat, slab, window, j):
    part = lax.dot_general(feat, slab, NT, preferred_element_type=F32)
    return part * window[:, j : j + 1]


def unit_kernel(
    early, tensor_far, pair_ref, feat_ref, window_ref,
    kept_ref, total_ref, both_ref, gram_ref, tensor_ref, sems,
):
    kept = kept_ref.shape[0]
    places = [
        (j, kept_ref.at[j] if j < kept else tensor_ref.at[j - kept]) for j in range(early)
    ]
    copies = fetches(tensor_far, places, sems)
    start(copies[0:5])
    pair = pair_ref[0:128].astype(F32)
    mine, other = feat_ref[...], pair[0:64] + pair[64:128]
    first = lax.axis_index("tm") == 0
    feat = jnp.concatenate(
        [jnp.where(first, mine, other), jnp.where(first, other, mine)], axis=-1
    )
    gram = lax.dot_general(feat, feat, NT, precision=HIGH, preferred_element_type=F32)
    place = lax.broadcasted_iota(jnp.int32, (64, 64), 0) // 16 == lax.axis_index("unit") // 4
    gram = jnp.sum(jnp.where(place, gram, 0.0).reshape(4, 16, 64), axis=0)
    gram_ref[...] = split(gram, -1).astype(BF16)
    both_ref[...] = low(feat)
    feat = feat.astype(BF16)
    window = low(window_ref[...]).T
    start(copies[5:])
    for j in range(early):
        for copy in copies[j]:
            copy.wait()
        add_to(total_ref, by_unit_part(feat, places[j][1][...], window, j), j == 0)


def feature_kernel(
    early, tensor_far, kept_ref, gather_ref, both_ref, window_ref, by_unit_ref,
    sums_ref, send_ref, keep_ref, tensor_ref, unit_ref, total, unit_total, products, sems,
):
    windows, kept = tensor_far.shape[0], kept_ref.shape[0]
    order = [*range(early, windows), *range(kept, early)]
    places = [(j, tensor_ref.at[at]) for at, j in enumerate(order)]
    copies = fetches(tensor_far, places, sems)
    start(copies[0:4])
    left = lax.broadcasted_iota(jnp.int32, (32, 128), 1) < 64
    for at in range(0, 16, 2):
        one = gather_ref[at].astype(F32)
        two = gather_ref[at + 1].astype(F32)
        columns = pl.ds(at * 64, 128)
        unit_ref[0:32, columns] = jnp.where(left, one, pltpu.roll(two, 64, 1)).astype(BF16)
        unit_ref[32:64, columns] = jnp.where(left, pltpu.roll(one, 64, 1), two).astype(BF16)
    unit = unit_ref[...]
    gram = lax.dot_general(unit, unit, NT, preferred_element_type=F32)
    both = both_ref[...]
    feat = both.astype(BF16)
    window = low(window_ref[...]).T
    unit_total[...] = by_unit_ref[...]

    def add_window(j, slab, fresh):
        second = jnp.dot(unit, slab, preferred_element_type=F32)
        product = second * both
        products[j] = product[:, :128] + product[:, 128:]
        add_to(total, second * window[:, j : j + 1], fresh)

    for j in range(kept):
        add_window(j, kept_ref[j], j == 0)
    start(copies[4:8])
    for at, j in enumerate(order):
        for copy in copies[at]:
            copy.wait()
        if at == 3:
            start(copies[8:])
        slab = tensor_ref[at]
        add_window(j, slab, False)
        if j >= early:
            add_to(unit_total, by_unit_part(feat, slab, window, j), False)
    first = lax.axis_index("tm") == 0
    for at in range(0, 16, 2):
        top = unit_total[0:32, at * 64 : at * 64 + 128]
        bottom = unit_total[32:64, at * 64 : at * 64 + 128]
        even = jnp.where(left, top, pltpu.roll(bottom, 64, 1))
        odd = jnp.where(left, pltpu.roll(top, 64, 1), bottom)
        send_ref[at // 2] = jnp.where(first, odd, even).astype(BF16)
        keep_ref[at // 2] = jnp.where(first, even, odd)
    rest = jnp.concatenate([spread(gram), spread(jnp.sum(products[...], axis=-1))], axis=0)
    parts = [total[:, :128], total[:, 128:], split(rest, 0)]
    sums_ref[...] = jnp.concatenate(parts, axis=0).astype(BF16)


def add_four(refs):
    one, two, three, four = [ref[...].astype(F32) for ref in refs]
    return (one + two) + (three + four)


def near_kernel(
    s0, s1, s2, s3, by_unit_ref, other_unit_ref, gram_ref, scatter_ref, send_ref, keep_ref
):
    total = add_four((s0, s1, s2, s3))
    rest = total[128:168] + total[168:208]
    first = lax.axis_index("tm") == 0
    send_ref[...] = jnp.where(first, total[64:128], total[0:64])
    keep_ref[0:64] = jnp.where(first, total[0:64], total[64:128])
    keep_ref[64:96] = rest[0:32]
    by_window = split(rest[32:40], 0).astype(BF16)
    for at in range(8):
        by_unit = by_unit_ref[at] + other_unit_ref[at].astype(F32)
        scatter_ref[at, 0:32] = by_unit.astype(BF16)
        scatter_ref[at, 32:48] = by_window
        scatter_ref[at, 48:64] = gram_ref[...]


def pair_kernel(keep_ref, other_ref, sums_ref):
    sums_ref[0:64] = keep_ref[0:64] + other_ref[...]
    sums_ref[64:96] = keep_ref[64:96]


def group_kernel(scatter_ref, keep_ref, unit_ref, sums_ref):
    total = scatter_ref[0].astype(F32)
    for at in range(1, 8):
        total += scatter_ref[at].astype(F32)
    unit_ref[...] = total[0:32]
    gram = total[48:64]
    gram = jnp.concatenate([gram[:, :64] + gram[:, 64:]] * 4, axis=0)
    place = lax.broadcasted_iota(jnp.int32, (64, 64), 0) // 16 == lax.axis_index("unit") // 4
    gram = spread(jnp.where(place, gram, 0.0))
    rest = jnp.concatenate([keep_ref[64:96], gram, total[32:40] + total[40:48]], axis=0)
    sums_ref[...] = jnp.concatenate([keep_ref[0:64], split(rest, 0)], axis=0).astype(BF16)


def gradient_kernel(
    scales, s0, s1, s2, s3, by_unit_ref, unit_ref, window_ref, feat_ref, pair_ref,
    grad_unit_ref, grad_window_ref, grad_feat_ref,
):
    total = add_four((s0, s1, s2, s3))
    rest = total[64:136] + total[136:208]
    gram_unit, gram_feat = stack(rest[0:32]), stack(rest[32:64])
    window = window_ref[...]
    other = pair_ref[128:144, :].astype(F32)
    other = other[:, :64] + other[:, 64:]
    windows = jnp.concatenate([window, other], axis=0)
    gram_window = lax.dot_general(
        windows, windows, TN, precision=HIGH, preferred_element_type=F32
    )
    grad_unit_ref[...] = (
        dot(unit_ref[...], gram_window * gram_feat) - stack(by_unit_ref[...]).T
    ) * scales[0]
    grad_window_ref[...] = (
        dot(window, gram_unit * gram_feat) - stack(rest[64:72])
    ) * scales[1]
    grad_feat_ref[...] = (dot(gram_unit * gram_window, feat_ref[...]) - total[0:64]) * scales[2]


NEAR = (1, 2, 3)
FAR = (8, 6, 14)


def by_xor(value, mask):
    count = lax.axis_size("unit")
    return lax.ppermute(value, "unit", [(i, i ^ mask) for i in range(count)])


def other_windows(value):
    count = lax.axis_size("unit") * lax.axis_size("tm")
    return lax.ppermute(value, ("unit", "tm"), [(i, i ^ 17) for i in range(count)])


def body(tensor, unit_factor, window_factor, feat_factor):
    win_rows, unit_count, feat_count = tensor.shape
    units_all = unit_count * lax.axis_size("unit")
    windows_all = win_rows * lax.axis_size("tm")
    feats_all = feat_count * lax.axis_size("feat")
    shape = jax.ShapeDtypeStruct
    feat = feat_factor.T
    gather, pair, feat_near, window_near = call(
        prepare_kernel,
        [
            shape((16, 32, 128), BF16),
            shape((144, 128), BF16),
            shape((64, 128), F32),
            shape((win_rows, 64), F32),
        ],
        unit_factor, feat, window_factor,
        far=(0, 1, 2),
        scratch_shapes=[pltpu.VMEM((64, 64), F32), pltpu.SemaphoreType.DMA((3,))],
        name="prepare",
    )
    pair = other_windows(pair)
    gather = lax.all_to_all(gather.reshape(512, 128), GROUP, 0, 0, tiled=True).reshape(16, 32, 128)
    cost = pl.CostEstimate(flops=2**33, bytes_accessed=2**23, transcendentals=0)
    kept, early = 5, 9
    slabs = functools.partial(pltpu.VMEM, dtype=BF16)
    kept_windows, by_unit, both, gram = call(
        functools.partial(unit_kernel, early),
        [
            slabs((kept, unit_count, feat_count)),
            shape((64, unit_count), F32),
            shape((64, feat_count), F32),
            shape((16, 128), BF16),
        ],
        tensor, pair, feat_near, window_near,
        far=(0,),
        scratch_shapes=[
            slabs((early - kept, unit_count, feat_count)),
            pltpu.SemaphoreType.DMA((2 * early,)),
        ],
        cost_estimate=cost,
        name="by_unit",
    )
    sums, send, by_unit = call(
        functools.partial(feature_kernel, early),
        [shape((208, 128), BF16), shape((8, 32, 128), BF16), shape((8, 32, 128), F32)],
        tensor, pltpu.with_memory_space_constraint(kept_windows, pltpu.VMEM),
        gather, both, window_near, by_unit,
        far=(0,),
        scratch_shapes=[
            slabs((win_rows - kept, unit_count, feat_count)),
            pltpu.VMEM((64, unit_count), BF16),
            pltpu.VMEM((64, feat_count), F32),
            pltpu.VMEM((64, unit_count), F32),
            pltpu.VMEM((win_rows, 64, 128), F32),
            pltpu.SemaphoreType.DMA((2 * win_rows,)),
        ],
        cost_estimate=cost,
        name="by_feature",
    )
    other_unit = lax.ppermute(send, "tm", [(0, 1), (1, 0)])
    near = [by_xor(sums, mask) for mask in NEAR]
    scatter, send, keep = call(
        near_kernel,
        [shape((8, 64, 128), BF16), shape((64, 128), F32), shape((96, 128), F32)],
        sums, *near, by_unit, other_unit, gram,
        name="near_sums",
    )
    other = other_windows(send)
    scatter = lax.all_to_all(scatter.reshape(512, 128), "feat", 0, 0, tiled=True).reshape(8, 64, 128)
    keep = call(pair_kernel, shape((96, 128), F32), keep, other, name="pair_sums")
    by_unit, sums = call(
        group_kernel,
        [shape((32, 128), F32), shape((208, 128), BF16)],
        scatter, keep,
        name="group_sums",
    )
    far = [by_xor(sums, mask) for mask in FAR]
    scales = (
        1 / math.sqrt(windows_all * feats_all),
        1 / math.sqrt(units_all * feats_all),
        1 / math.sqrt(units_all * windows_all),
    )
    grad_unit, grad_window, grad_feat = call(
        functools.partial(gradient_kernel, scales),
        [shape((64, 64), F32), shape((win_rows, 64), F32), shape((64, 128), F32)],
        sums, *far, by_unit, unit_factor, window_factor, feat, pair,
        name="gradients",
    )
    return grad_unit, grad_window, grad_feat.T


def solution(mesh):
    in_specs = (
        P("tm", "unit", "feat"),
        P(("unit", "feat", "tm"), None),
        P("tm", None),
        P(("feat", "tm"), None),
    )
    out_specs = (P(("unit", "feat", "tm"), None), P("tm", None), P(("feat", "tm"), None))
    return jax.shard_map(body, mesh=mesh, in_specs=in_specs, out_specs=out_specs, check_vma=False)
```

time: 67 us -> 59.8 us (0.89)
  starting transfers between devices: 28.2 us -> 23.8 us
  local copies, waits for them, and re-layouts: 3.54 us -> 0.01 us
  waiting for transfers between devices: 19.7 us -> 21.9 us
  Pallas kernels: 14.5 us -> 12.7 us
    all_to_all x1, waiting for transfers between devices: 3.42 us -> 7.26 us  [body(): lax.all_to_all(gather.reshape(512, 128), GROUP, 0, 0, tiled=True)]
    unnamed x10 -> x6, local copies, waits for them, and re-layouts: 3.54 us -> 0.01 us
    all_to_all x1, starting transfers between devices: 6.19 us -> 3.37 us  [body(): lax.all_to_all(scatter.reshape(512, 128), 'feat', 0, 0, tiled=True)]
    pallas_call x6 -> x7, Pallas kernels: 14.5 us -> 12.7 us  [call(): pl.pallas_call(kernel, out_shape=out_shape, in_specs=[HBM if at in far el...]
    all_to_all x1, waiting for transfers between devices: 6.95 us -> 5.33 us  [body(): lax.all_to_all(scatter.reshape(512, 128), 'feat', 0, 0, tiled=True)]
    ppermute x2 -> x3, starting transfers between devices: 5.64 us -> 4.7 us  [the longest x2 3.88 us: other_windows(): lax.ppermute(value, ('unit', 'tm'), [(i, i ^ 17) for i in range(count)])]
    ppermute x2 -> x3, waiting for transfers between devices: 2.23 us -> 1.9 us  [the longest x2 1.9 us: other_windows(): lax.ppermute(value, ('unit', 'tm'), [(i, i ^ 17) for i in range(count)])]
  transfers between devices with their start and end apart: 10 -> 11, of which waited for: 7 -> 7; matrix products, arithmetic and copies ran while one was open for 0% -> 0% of each run, Pallas kernels for 9% -> 7%
where the time goes in v2:
time: 59.8 us; the launch traced here: 59.1 us
  starting transfers between devices  23.8 us (40%)
  waiting for transfers between devices  21.9 us (37%)
  Pallas kernels  12.7 us (21%)
  between operations  0.7 us (1%)
    pallas_call x7, Pallas kernels, call(): pl.pallas_call(kernel, out_shape=out_shape, in_specs=[HBM if at in far el...  12.7 us
    all_to_all x1, starting transfers between devices, body(): lax.all_to_all(gather.reshape(512, 128), GROUP, 0, 0, tiled=True)  9.12 us
    ppermute x6, waiting for transfers between devices, by_xor(): return lax.ppermute(value, 'unit', [(i, i ^ mask) for i in range(count)])  7.43 us
    all_to_all x1, waiting for transfers between devices, body(): lax.all_to_all(gather.reshape(512, 128), GROUP, 0, 0, tiled=True)  7.26 us
    ppermute x6, starting transfers between devices, by_xor(): return lax.ppermute(value, 'unit', [(i, i ^ mask) for i in range(count)])  6.58 us
    all_to_all x1, waiting for transfers between devices, body(): lax.all_to_all(scatter.reshape(512, 128), 'feat', 0, 0, tiled=True)  5.33 us
    ppermute x2, starting transfers between devices, other_windows(): lax.ppermute(value, ('unit', 'tm'), [(i, i ^ 17) for i in range(count)])  3.88 us
    all_to_all x1, starting transfers between devices, body(): lax.all_to_all(scatter.reshape(512, 128), 'feat', 0, 0, tiled=True)  3.37 us
  transfers between devices with their start and end apart: 11, of which 7 were waited for; matrix products, arithmetic and copies ran while one was open for 0% of the time, Pallas kernels for 7%

profile of v2, /device:TPU:2, one launch (start us, length us, event | category | flops | bytes accessed | tf_op | source)
XLA Modules:
  0.0 59.1 jit_solution(12626316802829734827)
XLA Ops:
  0.6 1.7 %prepare.1 = (bf16[16,32,128]{2,1,0:T(8,128)(2,1)}, bf16[144,128]{1,0:T(8,128)(2,1)S(1)}, f32[64,128]{1,0:T(8,128)S(1)}, f32[16,64]{1,0:T(8,128)S(1)}) custom-call(f32[64,64]{1,0:T(8,128)} %unit_ref.1, f32[64,128]{1,0:T(8,128)} %bitcast.2, f32[16,64]{1,0:T(8,128)} %window_ref.1), custom_call_target="tpu_custom_call" | custom-call | tf_op jit(solution)/shard_map/prepare/pallas_call | solution.py:26
  2.3 1.6 %collective-permute-start = (bf16[144,128]{1,0:T(8,128)(2,1)S(1)}, bf16[144,128]{1,0:T(8,128)(2,1)S(1)}, u32[]{:S(2)}, u32[]{:S(2)}) collective-permute-start(bf16[144,128]{1,0:T(8,128)(2,1)S(1)} %get-tuple-element.22), channel_id=1, source_target_pairs={{0,129},{1,128},{16,145},{17,144},{32,161},{33,160},{48,177},{49,1... | collective-permute-start | bytes 110600 | tf_op jit(solution)/shard_map/ppermute | solution.py:268
  3.9 9.1 %all-to-all-start = ((bf16[16,32,128]{2,1,0:T(8,128)(2,1)}), bf16[16,32,128]{2,1,0:T(8,128)(2,1)S(1)}, u32[]{:S(2)}, u32[]{:S(2)}) async-start(bf16[16,32,128]{2,1,0:T(8,128)(2,1)} %get-tuple-element.26), calls=%async_computation | async-start | bytes 262144 | tf_op jit(solution)/shard_map/all_to_all | solution.py:292
  13.0 0.0 collective-permute-done.pair_ref
  13.0 3.8 %by_unit.1 = (bf16[5,1024,256]{2,1,0:T(8,128)(2,1)S(1)}, f32[64,1024]{1,0:T(8,128)S(1)}, f32[64,256]{1,0:T(8,128)S(1)}, bf16[16,128]{1,0:T(8,128)(2,1)S(1)}) custom-call(bf16[16,1024,256]{2,1,0:T(8,128)(2,1)} %tensor_far.3, bf16[144,128]{1,0:T(8,128)(2,1)S(1)} %collective-permute-done.pair_ref, f32[64,128]{1,0:T(8,128)S(1)} %get-tuple-element.23.feat_ref, ...), custom_call_target="tpu_custom_call" | custom-call | flops 8589934592 | bytes 8388608 | tf_op jit(solution)/shard_map/by_unit/pallas_call | solution.py:26
  16.9 7.3 %all-to-all-done.gather_ref = bf16[16,32,128]{2,1,0:T(8,128)(2,1)S(1)} async-done(((bf16[16,32,128]{2,1,0:T(8,128)(2,1)}), bf16[16,32,128]{2,1,0:T(8,128)(2,1)S(1)}, u32[]{:S(2)}, u32[]{:S(2)}) %all-to-all-start) | async-done | bytes 131104 | tf_op jit(solution)/shard_map/all_to_all | solution.py:292
  24.1 0.0 copy-start
  24.2 5.2 %by_feature.1 = (bf16[208,128]{1,0:T(8,128)(2,1)S(1)}, bf16[8,32,128]{2,1,0:T(8,128)(2,1)S(1)}, f32[8,32,128]{2,1,0:T(8,128)S(1)}) custom-call(bf16[16,1024,256]{2,1,0:T(8,128)(2,1)} %tensor_far.3, bf16[5,1024,256]{2,1,0:T(8,128)(2,1)S(1)} %get-tuple-element.25.kept_ref, bf16[16,32,128]{2,1,0:T(8,128)(2,1)S(1)} %all-to-all-done.gather_ref, ...), custom_call_target="tpu_custom_call" | custom-call | flops 8589934592 | bytes 8388608 | tf_op jit(solution)/shard_map/by_feature/pallas_call | solution.py:26
  29.3 0.8 %collective-permute-start.4 = (bf16[8,32,128]{2,1,0:T(8,128)(2,1)S(1)}, bf16[8,32,128]{2,1,0:T(8,128)(2,1)S(1)}, u32[]{:S(2)}, u32[]{:S(2)}) collective-permute-start(bf16[8,32,128]{2,1,0:T(8,128)(2,1)S(1)} %get-tuple-element.31), channel_id=1, source_target_pairs={{0,1},{1,0},{2,3},{3,2},{4,5},{5,4},{6,7},{7,6},{8,9},{9,8},{10,11... | collective-permute-start | bytes 196616 | tf_op jit(solution)/shard_map/ppermute | solution.py:330
  30.2 0.0 collective-permute-start.3
  30.2 1.6 %collective-permute-start.2 = (bf16[208,128]{1,0:T(8,128)(2,1)S(1)}, bf16[208,128]{1,0:T(8,128)(2,1)S(1)}, u32[]{:S(2)}, u32[]{:S(2)}) collective-permute-start(bf16[208,128]{1,0:T(8,128)(2,1)S(1)} %get-tuple-element.29.s0), channel_id=1, source_target_pairs={{0,32},{16,48},{32,0},{48,16},{64,96},{80,112},{96,64},{112,80},{1... | collective-permute-start | bytes 159752 | tf_op jit(solution)/shard_map/ppermute | solution.py:263
  31.8 0.3 collective-permute-start.1
  32.0 2.1 %collective-permute-done.3.s3 = bf16[208,128]{1,0:T(8,128)(2,1)S(1)} collective-permute-done((bf16[208,128]{1,0:T(8,128)(2,1)S(1)}, bf16[208,128]{1,0:T(8,128)(2,1)S(1)}, u32[]{:S(2)}, u32[]{:S(2)}) %collective-permute-start.3) | collective-permute-done | bytes 53280 | tf_op jit(solution)/shard_map/ppermute | solution.py:263
  34.2 1.1 %collective-permute-done.2.s2 = bf16[208,128]{1,0:T(8,128)(2,1)S(1)} collective-permute-done((bf16[208,128]{1,0:T(8,128)(2,1)S(1)}, bf16[208,128]{1,0:T(8,128)(2,1)S(1)}, u32[]{:S(2)}, u32[]{:S(2)}) %collective-permute-start.2) | collective-permute-done | bytes 53280 | tf_op jit(solution)/shard_map/ppermute | solution.py:263
  35.3 0.0 collective-permute-done.1.s1
  35.3 0.0 collective-permute-done.4.other_unit_ref
  35.3 0.7 %near_sums.1 = (bf16[8,64,128]{2,1,0:T(8,128)(2,1)}, f32[64,128]{1,0:T(8,128)S(1)}, f32[96,128]{1,0:T(8,128)S(1)}) custom-call(bf16[208,128]{1,0:T(8,128)(2,1)S(1)} %get-tuple-element.29.s0, bf16[208,128]{1,0:T(8,128)(2,1)S(1)} %collective-permute-done.1.s1, bf16[208,128]{1,0:T(8,128)(2,1)S(1)} %collective-permute-done.2.s2, ...), custom_call_target="tpu_custom_call" | custom-call | tf_op jit(solution)/shard_map/near_sums/pallas_call | solution.py:26
  35.9 3.4 %all-to-all-start.1 = ((bf16[8,64,128]{2,1,0:T(8,128)(2,1)}), bf16[8,64,128]{2,1,0:T(8,128)(2,1)S(1)}, u32[]{:S(2)}, u32[]{:S(2)}) async-start(bf16[8,64,128]{2,1,0:T(8,128)(2,1)} %get-tuple-element.33), calls=%async_computation.1 | async-start | bytes 262144 | tf_op jit(solution)/shard_map/all_to_all | solution.py:339
  39.3 2.3 %collective-permute-start.5 = (f32[64,128]{1,0:T(8,128)S(1)}, f32[64,128]{1,0:T(8,128)S(1)}, u32[]{:S(2)}, u32[]{:S(2)}) collective-permute-start(f32[64,128]{1,0:T(8,128)S(1)} %get-tuple-element.35), channel_id=1, source_target_pairs={{0,129},{1,128},{16,145},{17,144},{32,161},{33,160},{48,177},{49,1... | collective-permute-start | bytes 98312 | tf_op jit(solution)/shard_map/ppermute | solution.py:268
  41.6 1.9 %collective-permute-done.5.other_ref = f32[64,128]{1,0:T(8,128)S(1)} collective-permute-done((f32[64,128]{1,0:T(8,128)S(1)}, f32[64,128]{1,0:T(8,128)S(1)}, u32[]{:S(2)}, u32[]{:S(2)}) %collective-permute-start.5) | collective-permute-done | bytes 32800 | tf_op jit(solution)/shard_map/ppermute | solution.py:268
  43.5 5.3 %all-to-all-done.1.scatter_ref = bf16[8,64,128]{2,1,0:T(8,128)(2,1)S(1)} async-done(((bf16[8,64,128]{2,1,0:T(8,128)(2,1)}), bf16[8,64,128]{2,1,0:T(8,128)(2,1)S(1)}, u32[]{:S(2)}, u32[]{:S(2)}) %all-to-all-start.1) | async-done | bytes 131104 | tf_op jit(solution)/shard_map/all_to_all | solution.py:339
  48.8 0.2 group_sums.1
  49.0 3.6 %collective-permute-start.8 = (bf16[208,128]{1,0:T(8,128)(2,1)S(1)}, bf16[208,128]{1,0:T(8,128)(2,1)S(1)}, u32[]{:S(2)}, u32[]{:S(2)}) collective-permute-start(bf16[208,128]{1,0:T(8,128)(2,1)S(1)} %get-tuple-element.36.s0), channel_id=1, source_target_pairs={{0,224},{16,240},{32,192},{48,208},{64,160},{80,176},{96,128},{112... | collective-permute-start | bytes 159752 | tf_op jit(solution)/shard_map/ppermute | solution.py:263
  52.6 0.6 %collective-permute-start.7 = (bf16[208,128]{1,0:T(8,128)(2,1)S(1)}, bf16[208,128]{1,0:T(8,128)(2,1)S(1)}, u32[]{:S(2)}, u32[]{:S(2)}) collective-permute-start(bf16[208,128]{1,0:T(8,128)(2,1)S(1)} %get-tuple-element.36.s0), channel_id=1, source_target_pairs={{0,96},{16,112},{32,64},{48,80},{64,32},{80,48},{96,0},{112,16},{1... | collective-permute-start | bytes 159752 | tf_op jit(solution)/shard_map/ppermute | solution.py:263
  53.2 0.5 collective-permute-start.6
  53.7 1.7 %collective-permute-done.8.s3 = bf16[208,128]{1,0:T(8,128)(2,1)S(1)} collective-permute-done((bf16[208,128]{1,0:T(8,128)(2,1)S(1)}, bf16[208,128]{1,0:T(8,128)(2,1)S(1)}, u32[]{:S(2)}, u32[]{:S(2)}) %collective-permute-start.8) | collective-permute-done | bytes 53280 | tf_op jit(solution)/shard_map/ppermute | solution.py:263
  55.4 2.5 %collective-permute-done.7.s2 = bf16[208,128]{1,0:T(8,128)(2,1)S(1)} collective-permute-done((bf16[208,128]{1,0:T(8,128)(2,1)S(1)}, bf16[208,128]{1,0:T(8,128)(2,1)S(1)}, u32[]{:S(2)}, u32[]{:S(2)}) %collective-permute-start.7) | collective-permute-done | bytes 53280 | tf_op jit(solution)/shard_map/ppermute | solution.py:263
  57.9 0.0 collective-permute-done.6.s1
  57.9 0.0 copy-done
  57.9 0.0 copy-done.1
  57.9 0.0 copy-done.2
  58.0 1.2 %gradients.1 = (f32[64,64]{1,0:T(8,128)}, f32[16,64]{1,0:T(8,128)}, f32[64,128]{1,0:T(8,128)}) custom-call(bf16[208,128]{1,0:T(8,128)(2,1)S(1)} %get-tuple-element.36.s0, bf16[208,128]{1,0:T(8,128)(2,1)S(1)} %collective-permute-done.6.s1, bf16[208,128]{1,0:T(8,128)(2,1)S(1)} %collective-permute-done.7.s2, bf16[208,128]{1,0:T(8,128)(2,1)S(1)} %collective-permute-done.8.s3, ...), custom_call_target="tpu_custom_call" | custom-call | tf_op jit(solution)/shard_map/gradients/pallas_call | solution.py:26
  (3 shorter events, 0.0 us)
Async XLA Ops:
  2.3 10.7 %collective-permute-start = (bf16[144,128]{1,0:T(8,128)(2,1)S(1)}, bf16[144,128]{1,0:T(8,128)(2,1)S(1)}, u32[]{:S(2)}, u32[]{:S(2)}) collective-permute-start(bf16[144,128]{1,0:T(8,128)(2,1)S(1)} %get-tuple-element.22), channel_id=1, source_target_pairs={{0,129},{1,128},{16,145},{17,144},{32,161},{33,160},{48,177},{49,1... | collective-permute-start | bytes 110600 | tf_op jit(solution)/shard_map/ppermute | solution.py:268
  3.9 20.2 %all-to-all-start = ((bf16[16,32,128]{2,1,0:T(8,128)(2,1)}), bf16[16,32,128]{2,1,0:T(8,128)(2,1)S(1)}, u32[]{:S(2)}, u32[]{:S(2)}) async-start(bf16[16,32,128]{2,1,0:T(8,128)(2,1)} %get-tuple-element.26), calls=%async_computation | async-start | bytes 262144 | tf_op jit(solution)/shard_map/all_to_all | solution.py:292
  24.1 33.8 %copy-start = (f32[64,64]{1,0:T(8,128)S(1)}, f32[64,64]{1,0:T(8,128)}, u32[]{:S(2)}) copy-start(f32[64,64]{1,0:T(8,128)} %unit_ref.1) | copy-start | bytes 49156
  24.2 33.8 %copy-start.1 = (f32[128,64]{0,1:T(8,128)S(1)}, f32[128,64]{0,1:T(8,128)}, u32[]{:S(2)}) copy-start(f32[128,64]{0,1:T(8,128)} %param.7) | copy-start | bytes 98308
  24.2 33.8 %copy-start.2 = (f32[16,64]{1,0:T(8,128)S(1)}, f32[16,64]{1,0:T(8,128)}, u32[]{:S(2)}) copy-start(f32[16,64]{1,0:T(8,128)} %window_ref.1) | copy-start | bytes 12292
  29.3 5.9 %collective-permute-start.4 = (bf16[8,32,128]{2,1,0:T(8,128)(2,1)S(1)}, bf16[8,32,128]{2,1,0:T(8,128)(2,1)S(1)}, u32[]{:S(2)}, u32[]{:S(2)}) collective-permute-start(bf16[8,32,128]{2,1,0:T(8,128)(2,1)S(1)} %get-tuple-element.31), channel_id=1, source_target_pairs={{0,1},{1,0},{2,3},{3,2},{4,5},{5,4},{6,7},{7,6},{8,9},{9,8},{10,11... | collective-permute-start | bytes 196616 | tf_op jit(solution)/shard_map/ppermute | solution.py:330
  30.2 4.0 %collective-permute-start.3 = (bf16[208,128]{1,0:T(8,128)(2,1)S(1)}, bf16[208,128]{1,0:T(8,128)(2,1)S(1)}, u32[]{:S(2)}, u32[]{:S(2)}) collective-permute-start(bf16[208,128]{1,0:T(8,128)(2,1)S(1)} %get-tuple-element.29.s0), channel_id=1, source_target_pairs={{0,48},{16,32},{32,16},{48,0},{64,112},{80,96},{96,80},{112,64},{1... | collective-permute-start | bytes 159752 | tf_op jit(solution)/shard_map/ppermute | solution.py:263
  30.2 5.1 %collective-permute-start.2 = (bf16[208,128]{1,0:T(8,128)(2,1)S(1)}, bf16[208,128]{1,0:T(8,128)(2,1)S(1)}, u32[]{:S(2)}, u32[]{:S(2)}) collective-permute-start(bf16[208,128]{1,0:T(8,128)(2,1)S(1)} %get-tuple-element.29.s0), channel_id=1, source_target_pairs={{0,32},{16,48},{32,0},{48,16},{64,96},{80,112},{96,64},{112,80},{1... | collective-permute-start | bytes 159752 | tf_op jit(solution)/shard_map/ppermute | solution.py:263
  31.8 3.5 %collective-permute-start.1 = (bf16[208,128]{1,0:T(8,128)(2,1)S(1)}, bf16[208,128]{1,0:T(8,128)(2,1)S(1)}, u32[]{:S(2)}, u32[]{:S(2)}) collective-permute-start(bf16[208,128]{1,0:T(8,128)(2,1)S(1)} %get-tuple-element.29.s0), channel_id=1, source_target_pairs={{0,16},{16,0},{32,48},{48,32},{64,80},{80,64},{96,112},{112,96},{1... | collective-permute-start | bytes 159752 | tf_op jit(solution)/shard_map/ppermute | solution.py:263
  35.9 12.9 %all-to-all-start.1 = ((bf16[8,64,128]{2,1,0:T(8,128)(2,1)}), bf16[8,64,128]{2,1,0:T(8,128)(2,1)S(1)}, u32[]{:S(2)}, u32[]{:S(2)}) async-start(bf16[8,64,128]{2,1,0:T(8,128)(2,1)} %get-tuple-element.33), calls=%async_computation.1 | async-start | bytes 262144 | tf_op jit(solution)/shard_map/all_to_all | solution.py:339
  39.3 4.2 %collective-permute-start.5 = (f32[64,128]{1,0:T(8,128)S(1)}, f32[64,128]{1,0:T(8,128)S(1)}, u32[]{:S(2)}, u32[]{:S(2)}) collective-permute-start(f32[64,128]{1,0:T(8,128)S(1)} %get-tuple-element.35), channel_id=1, source_target_pairs={{0,129},{1,128},{16,145},{17,144},{32,161},{33,160},{48,177},{49,1... | collective-permute-start | bytes 98312 | tf_op jit(solution)/shard_map/ppermute | solution.py:268
  49.0 6.4 %collective-permute-start.8 = (bf16[208,128]{1,0:T(8,128)(2,1)S(1)}, bf16[208,128]{1,0:T(8,128)(2,1)S(1)}, u32[]{:S(2)}, u32[]{:S(2)}) collective-permute-start(bf16[208,128]{1,0:T(8,128)(2,1)S(1)} %get-tuple-element.36.s0), channel_id=1, source_target_pairs={{0,224},{16,240},{32,192},{48,208},{64,160},{80,176},{96,128},{112... | collective-permute-start | bytes 159752 | tf_op jit(solution)/shard_map/ppermute | solution.py:263
  52.6 5.3 %collective-permute-start.7 = (bf16[208,128]{1,0:T(8,128)(2,1)S(1)}, bf16[208,128]{1,0:T(8,128)(2,1)S(1)}, u32[]{:S(2)}, u32[]{:S(2)}) collective-permute-start(bf16[208,128]{1,0:T(8,128)(2,1)S(1)} %get-tuple-element.36.s0), channel_id=1, source_target_pairs={{0,96},{16,112},{32,64},{48,80},{64,32},{80,48},{96,0},{112,16},{1... | collective-permute-start | bytes 159752 | tf_op jit(solution)/shard_map/ppermute | solution.py:263
  53.2 4.7 %collective-permute-start.6 = (bf16[208,128]{1,0:T(8,128)(2,1)S(1)}, bf16[208,128]{1,0:T(8,128)(2,1)S(1)}, u32[]{:S(2)}, u32[]{:S(2)}) collective-permute-start(bf16[208,128]{1,0:T(8,128)(2,1)S(1)} %get-tuple-element.36.s0), channel_id=1, source_target_pairs={{0,128},{16,144},{32,160},{48,176},{64,192},{80,208},{96,224},{112... | collective-permute-start | bytes 159752 | tf_op jit(solution)/shard_map/ppermute | solution.py:263

commit v3 on v2

--- a/solution.py
+++ b/solution.py
@@ -14,6 +14,7 @@
 NT = (((1,), (1,)), ((), ()))
 TN = (((0,), (0,)), ((), ()))
 GROUP = ("feat", "tm")
+FAR = (8, 6, 14)
 VMEM = pl.BlockSpec(memory_space=pltpu.VMEM)
 HBM = pl.BlockSpec(memory_space=pltpu.HBM)
 
@@ -56,26 +57,6 @@
     return jnp.dot(one, two, precision=HIGH, preferred_element_type=F32)
 
 
-def prepare_kernel(
-    unit_far, feat_far, window_far, gather_ref, pair_ref, feat_ref, window_ref, unit_ref, sems
-):
-    copies = [
-        pltpu.make_async_copy(unit_far, unit_ref, sems.at[0]),
-        pltpu.make_async_copy(feat_far, feat_ref, sems.at[1]),
-        pltpu.make_async_copy(window_far, window_ref, sems.at[2]),
-    ]
-    for copy in copies:
-        copy.start()
-    copies[1].wait()
-    copies[2].wait()
-    parts = [split(feat_ref[...], 0), split(window_ref[...], -1)]
-    pair_ref[...] = jnp.concatenate(parts, axis=0).astype(BF16)
-    copies[0].wait()
-    chunk = spread(unit_ref[...].T).astype(BF16)
-    for at in range(16):
-        gather_ref[at] = chunk
-
-
 def fetches(tensor_far, places, sems):
     rows = tensor_far.shape[1] // 2
     result = []
@@ -95,6 +76,11 @@
             copy.start()
 
 
+def in_turn(steps):
+    for step in steps:
+        pl.when(lax.axis_index("tm") >= 0)(step)
+
+
 def add_to(total, part, fresh):
     if fresh:
         total[...] = part
@@ -108,17 +94,24 @@
 
 
 def unit_kernel(
-    early, tensor_far, pair_ref, feat_ref, window_ref,
-    kept_ref, total_ref, both_ref, gram_ref, tensor_ref, sems,
+    early, tensor_far, other_ref, feat_far, window_far,
+    kept_ref, total_ref, both_ref, gram_ref, window_ref, feat_ref, tensor_ref, sems, own_sems,
 ):
+    own = [
+        pltpu.make_async_copy(feat_far, feat_ref, own_sems.at[0]),
+        pltpu.make_async_copy(window_far, window_ref, own_sems.at[1]),
+    ]
+    for copy in own:
+        copy.start()
     kept = kept_ref.shape[0]
     places = [
         (j, kept_ref.at[j] if j < kept else tensor_ref.at[j - kept]) for j in range(early)
     ]
     copies = fetches(tensor_far, places, sems)
-    start(copies[0:5])
-    pair = pair_ref[0:128].astype(F32)
-    mine, other = feat_ref[...], pair[0:64] + pair[64:128]
+    start(copies[0:4])
+    for copy in own:
+        copy.wait()
+    mine, other = feat_ref[...], other_ref[...]
     first = lax.axis_index("tm") == 0
     feat = jnp.concatenate(
         [jnp.where(first, mine, other), jnp.where(first, other, mine)], axis=-1
@@ -130,11 +123,16 @@
     both_ref[...] = low(feat)
     feat = feat.astype(BF16)
     window = low(window_ref[...]).T
-    start(copies[5:])
-    for j in range(early):
-        for copy in copies[j]:
-            copy.wait()
-        add_to(total_ref, by_unit_part(feat, places[j][1][...], window, j), j == 0)
+    start(copies[4:])
+
+    def some(first, last):
+        for j in range(first, last):
+            for copy in copies[j]:
+                copy.wait()
+        for j in range(first, last):
+            add_to(total_ref, by_unit_part(feat, places[j][1][...], window, j), j == 0)
+
+    in_turn([functools.partial(some, 0, 4), functools.partial(some, 4, early)])
 
 
 def feature_kernel(
@@ -148,11 +146,9 @@
     start(copies[0:4])
     left = lax.broadcasted_iota(jnp.int32, (32, 128), 1) < 64
     for at in range(0, 16, 2):
-        one = gather_ref[at].astype(F32)
-        two = gather_ref[at + 1].astype(F32)
-        columns = pl.ds(at * 64, 128)
-        unit_ref[0:32, columns] = jnp.where(left, one, pltpu.roll(two, 64, 1)).astype(BF16)
-        unit_ref[32:64, columns] = jnp.where(left, pltpu.roll(one, 64, 1), two).astype(BF16)
+        rows = [stack(gather_ref[at].astype(F32)), stack(gather_ref[at + 1].astype(F32))]
+        unit_ref[:, pl.ds(at * 64, 128)] = jnp.concatenate(rows, axis=0).T.astype(BF16)
+    start(copies[4:8])
     unit = unit_ref[...]
     gram = lax.dot_general(unit, unit, NT, preferred_element_type=F32)
     both = both_ref[...]
@@ -166,18 +162,22 @@
         products[j] = product[:, :128] + product[:, 128:]
         add_to(total, second * window[:, j : j + 1], fresh)
 
-    for j in range(kept):
-        add_window(j, kept_ref[j], j == 0)
-    start(copies[4:8])
-    for at, j in enumerate(order):
-        for copy in copies[at]:
-            copy.wait()
-        if at == 3:
-            start(copies[8:])
-        slab = tensor_ref[at]
-        add_window(j, slab, False)
-        if j >= early:
-            add_to(unit_total, by_unit_part(feat, slab, window, j), False)
+    def held():
+        start(copies[8:])
+        for j in range(kept):
+            add_window(j, kept_ref[j], j == 0)
+
+    def some(first, last):
+        for at in range(first, last):
+            for copy in copies[at]:
+                copy.wait()
+        for at in range(first, last):
+            slab, j = tensor_ref[at], order[at]
+            add_window(j, slab, False)
+            if j >= early:
+                add_to(unit_total, by_unit_part(feat, slab, window, j), False)
+
+    in_turn([held, functools.partial(some, 0, 5), functools.partial(some, 5, len(order))])
     first = lax.axis_index("tm") == 0
     for at in range(0, 16, 2):
         top = unit_total[0:32, at * 64 : at * 64 + 128]
@@ -191,18 +191,25 @@
     sums_ref[...] = jnp.concatenate(parts, axis=0).astype(BF16)
 
 
-def add_four(refs):
-    one, two, three, four = [ref[...].astype(F32) for ref in refs]
+def add_four(values):
+    one, two, three, four = values
     return (one + two) + (three + four)
 
 
+def join_kernel(s0, s1, sums_ref):
+    total = s0[...].astype(F32) + s1[...].astype(F32)
+    rest = split(total[128:168] + total[168:208], 0)
+    sums_ref[...] = jnp.concatenate([total[0:128], rest], axis=0).astype(BF16)
+
+
 def near_kernel(
-    s0, s1, s2, s3, by_unit_ref, other_unit_ref, gram_ref, scatter_ref, send_ref, keep_ref
+    s0, s1, by_unit_ref, other_unit_ref, gram_ref, window_ref, scatter_ref, send_ref, keep_ref
 ):
-    total = add_four((s0, s1, s2, s3))
+    total = s0[...].astype(F32) + s1[...].astype(F32)
     rest = total[128:168] + total[168:208]
     first = lax.axis_index("tm") == 0
-    send_ref[...] = jnp.where(first, total[64:128], total[0:64])
+    send_ref[0:64] = jnp.where(first, total[64:128], total[0:64])
+    send_ref[64:72] = spread(window_ref[...])
     keep_ref[0:64] = jnp.where(first, total[0:64], total[64:128])
     keep_ref[64:96] = rest[0:32]
     by_window = split(rest[32:40], 0).astype(BF16)
@@ -213,8 +220,12 @@
         scatter_ref[at, 48:64] = gram_ref[...]
 
 
-def pair_kernel(keep_ref, other_ref, sums_ref):
-    sums_ref[0:64] = keep_ref[0:64] + other_ref[...]
+def pair_kernel(keep_ref, other_ref, window_ref, sums_ref, gram_ref):
+    windows = jnp.concatenate([window_ref[...], stack(other_ref[64:72])], axis=0)
+    gram_ref[...] = lax.dot_general(
+        windows, windows, TN, precision=HIGH, preferred_element_type=F32
+    )
+    sums_ref[0:64] = keep_ref[0:64] + other_ref[0:64]
     sums_ref[64:96] = keep_ref[64:96]
 
 
@@ -223,39 +234,33 @@
     for at in range(1, 8):
         total += scatter_ref[at].astype(F32)
     unit_ref[...] = total[0:32]
-    gram = total[48:64]
-    gram = jnp.concatenate([gram[:, :64] + gram[:, 64:]] * 4, axis=0)
-    place = lax.broadcasted_iota(jnp.int32, (64, 64), 0) // 16 == lax.axis_index("unit") // 4
-    gram = spread(jnp.where(place, gram, 0.0))
-    rest = jnp.concatenate([keep_ref[64:96], gram, total[32:40] + total[40:48]], axis=0)
+    gram = spread(total[48:64, :64] + total[48:64, 64:])
+    rest = jnp.concatenate([keep_ref[64:96], total[32:40] + total[40:48], gram], axis=0)
     sums_ref[...] = jnp.concatenate([keep_ref[0:64], split(rest, 0)], axis=0).astype(BF16)
 
 
 def gradient_kernel(
-    scales, s0, s1, s2, s3, by_unit_ref, unit_ref, window_ref, feat_ref, pair_ref,
+    scales, s0, s1, s2, s3, by_unit_ref, unit_ref, window_ref, feat_ref, gram_window_ref,
     grad_unit_ref, grad_window_ref, grad_feat_ref,
 ):
-    total = add_four((s0, s1, s2, s3))
-    rest = total[64:136] + total[136:208]
-    gram_unit, gram_feat = stack(rest[0:32]), stack(rest[32:64])
+    parts = [ref[...].astype(F32) for ref in (s0, s1, s2, s3)]
+    total = add_four(parts)
+    rest = total[64:112] + total[112:160]
+    gram_unit = stack(rest[0:32])
+    gram_feat = jnp.zeros((64, 64), F32)
+    place = lax.broadcasted_iota(jnp.int32, (64, 64), 0) // 16
+    for part, mask in zip(parts, (0, *FAR)):
+        rows = jnp.concatenate([stack(part[104:112] + part[152:160])] * 4, axis=0)
+        gram_feat = jnp.where(place == (lax.axis_index("unit") ^ mask) // 4, rows, gram_feat)
     window = window_ref[...]
-    other = pair_ref[128:144, :].astype(F32)
-    other = other[:, :64] + other[:, 64:]
-    windows = jnp.concatenate([window, other], axis=0)
-    gram_window = lax.dot_general(
-        windows, windows, TN, precision=HIGH, preferred_element_type=F32
-    )
+    gram_window = gram_window_ref[...]
     grad_unit_ref[...] = (
         dot(unit_ref[...], gram_window * gram_feat) - stack(by_unit_ref[...]).T
     ) * scales[0]
     grad_window_ref[...] = (
-        dot(window, gram_unit * gram_feat) - stack(rest[64:72])
+        dot(window, gram_unit * gram_feat) - stack(rest[32:40])
     ) * scales[1]
     grad_feat_ref[...] = (dot(gram_unit * gram_window, feat_ref[...]) - total[0:64]) * scales[2]
-
-
-NEAR = (1, 2, 3)
-FAR = (8, 6, 14)
 
 
 def by_xor(value, mask):
@@ -275,37 +280,27 @@
     feats_all = feat_count * lax.axis_size("feat")
     shape = jax.ShapeDtypeStruct
     feat = feat_factor.T
-    gather, pair, feat_near, window_near = call(
-        prepare_kernel,
-        [
-            shape((16, 32, 128), BF16),
-            shape((144, 128), BF16),
-            shape((64, 128), F32),
-            shape((win_rows, 64), F32),
-        ],
-        unit_factor, feat, window_factor,
-        far=(0, 1, 2),
-        scratch_shapes=[pltpu.VMEM((64, 64), F32), pltpu.SemaphoreType.DMA((3,))],
-        name="prepare",
-    )
-    pair = other_windows(pair)
+    gather = jnp.broadcast_to(spread(unit_factor.astype(BF16)), (16, 32, 128))
     gather = lax.all_to_all(gather.reshape(512, 128), GROUP, 0, 0, tiled=True).reshape(16, 32, 128)
     cost = pl.CostEstimate(flops=2**33, bytes_accessed=2**23, transcendentals=0)
-    kept, early = 5, 9
+    kept, early = 5, 8
     slabs = functools.partial(pltpu.VMEM, dtype=BF16)
-    kept_windows, by_unit, both, gram = call(
+    kept_windows, by_unit, both, gram, window_near = call(
         functools.partial(unit_kernel, early),
         [
             slabs((kept, unit_count, feat_count)),
             shape((64, unit_count), F32),
             shape((64, feat_count), F32),
             shape((16, 128), BF16),
+            shape((win_rows, 64), F32),
         ],
-        tensor, pair, feat_near, window_near,
-        far=(0,),
+        tensor, other_windows(feat), feat, window_factor,
+        far=(0, 2, 3),
         scratch_shapes=[
+            pltpu.VMEM((64, 128), F32),
             slabs((early - kept, unit_count, feat_count)),
             pltpu.SemaphoreType.DMA((2 * early,)),
+            pltpu.SemaphoreType.DMA((2,)),
         ],
         cost_estimate=cost,
         name="by_unit",
@@ -328,19 +323,24 @@
         name="by_feature",
     )
     other_unit = lax.ppermute(send, "tm", [(0, 1), (1, 0)])
-    near = [by_xor(sums, mask) for mask in NEAR]
+    sums = call(join_kernel, shape((208, 128), BF16), sums, by_xor(sums, 1), name="pair_sums")
     scatter, send, keep = call(
         near_kernel,
-        [shape((8, 64, 128), BF16), shape((64, 128), F32), shape((96, 128), F32)],
-        sums, *near, by_unit, other_unit, gram,
+        [shape((8, 64, 128), BF16), shape((72, 128), F32), shape((96, 128), F32)],
+        sums, by_xor(sums, 2), by_unit, other_unit, gram, window_near,
         name="near_sums",
     )
     other = other_windows(send)
     scatter = lax.all_to_all(scatter.reshape(512, 128), "feat", 0, 0, tiled=True).reshape(8, 64, 128)
-    keep = call(pair_kernel, shape((96, 128), F32), keep, other, name="pair_sums")
+    keep, gram_window = call(
+        pair_kernel,
+        [shape((96, 128), F32), shape((64, 64), F32)],
+        keep, other, window_near,
+        name="other_sums",
+    )
     by_unit, sums = call(
         group_kernel,
-        [shape((32, 128), F32), shape((208, 128), BF16)],
+        [shape((32, 128), F32), shape((160, 128), BF16)],
         scatter, keep,
         name="group_sums",
     )
@@ -353,7 +353,7 @@
     grad_unit, grad_window, grad_feat = call(
         functools.partial(gradient_kernel, scales),
         [shape((64, 64), F32), shape((win_rows, 64), F32), shape((64, 128), F32)],
-        sums, *far, by_unit, unit_factor, window_factor, feat, pair,
+        sums, *far, by_unit, unit_factor, window_factor, feat, gram_window,
         name="gradients",
     )
     return grad_unit, grad_window, grad_feat.T

time: 59.8 us -> 59 us (0.987)
  Pallas kernels: 12.7 us -> 11 us
  starting transfers between devices: 23.8 us -> 22.7 us
  other arithmetic: 0 us -> 0.84 us
  waiting for transfers between devices: 21.9 us -> 22.7 us
  local copies, waits for them, and re-layouts: 0.01 us -> 0.68 us
    ppermute x1, waiting for transfers between devices: 0.01 us -> 3.11 us  [body(): other_unit = lax.ppermute(send, 'tm', [(0, 1), (1, 0)])]
    ppermute x6 -> x5, waiting for transfers between devices: 7.43 us -> 4.86 us  [by_xor(): return lax.ppermute(value, 'unit', [(i, i ^ mask) for i in range(count)])]
    pallas_call x7, Pallas kernels: 12.7 us -> 11 us  [call(): pl.pallas_call(kernel, out_shape=out_shape, in_specs=[HBM if at in far el...]
    ppermute x2, starting transfers between devices: 3.88 us -> 2.93 us  [other_windows(): lax.ppermute(value, ('unit', 'tm'), [(i, i ^ 17) for i in range(count)])]
    ppermute x2, waiting for transfers between devices: 1.9 us -> 2.7 us  [other_windows(): lax.ppermute(value, ('unit', 'tm'), [(i, i ^ 17) for i in range(count)])]
    convert_element_type x0 -> x1, other arithmetic: none -> 0.76 us  [body(): gather = jnp.broadcast_to(spread(unit_factor.astype(BF16)), (16, 32, 128))]
    broadcast_in_dim x0 -> x1, local copies, waits for them, and re-layouts: none -> 0.67 us  [body(): gather = jnp.broadcast_to(spread(unit_factor.astype(BF16)), (16, 32, 128))]
    ppermute x6 -> x5, starting transfers between devices: 6.58 us -> 6.45 us  [by_xor(): return lax.ppermute(value, 'unit', [(i, i ^ mask) for i in range(count)])]
  transfers between devices with their start and end apart: 11 -> 10, of which waited for: 7 -> 7; matrix products, arithmetic and copies ran while one was open for 0% -> 3% of each run, Pallas kernels for 7% -> 7%
where the time goes in v3:
time: 59 us; the launch traced here: 58.6 us
  starting transfers between devices  22.7 us (38%)
  waiting for transfers between devices  22.7 us (38%)
  Pallas kernels  11 us (19%)
  other arithmetic  0.84 us (1%)
  between operations  0.71 us (1%)
  local copies, waits for them, and re-layouts  0.68 us (1%)
    pallas_call x7, Pallas kernels, call(): pl.pallas_call(kernel, out_shape=out_shape, in_specs=[HBM if at in far el...  11 us
    all_to_all x1, starting transfers between devices, body(): lax.all_to_all(gather.reshape(512, 128), GROUP, 0, 0, tiled=True)  9.12 us
    all_to_all x1, waiting for transfers between devices, body(): lax.all_to_all(gather.reshape(512, 128), GROUP, 0, 0, tiled=True)  7.28 us
    ppermute x5, starting transfers between devices, by_xor(): return lax.ppermute(value, 'unit', [(i, i ^ mask) for i in range(count)])  6.45 us
    ppermute x5, waiting for transfers between devices, by_xor(): return lax.ppermute(value, 'unit', [(i, i ^ mask) for i in range(count)])  4.86 us
    all_to_all x1, waiting for transfers between devices, body(): lax.all_to_all(scatter.reshape(512, 128), 'feat', 0, 0, tiled=True)  4.74 us
    all_to_all x1, starting transfers between devices, body(): lax.all_to_all(scatter.reshape(512, 128), 'feat', 0, 0, tiled=True)  3.37 us
    ppermute x1, waiting for transfers between devices, body(): other_unit = lax.ppermute(send, 'tm', [(0, 1), (1, 0)])  3.11 us
  transfers between devices with their start and end apart: 10, of which 7 were waited for; matrix products, arithmetic and copies ran while one was open for 3% of the time, Pallas kernels for 7%

profile of v3, /device:TPU:2, one launch (start us, length us, event | category | flops | bytes accessed | tf_op | source)
XLA Modules:
  0.0 58.6 jit_solution(1094395689565379771)
XLA Ops:
  0.6 1.6 %collective-permute-start = (f32[64,128]{1,0:T(8,128)}, f32[64,128]{1,0:T(8,128)S(1)}, u32[]{:S(2)}, u32[]{:S(2)}) collective-permute-start(f32[64,128]{1,0:T(8,128)} %bitcast.2), channel_id=1, source_target_pairs={{0,129},{1,128},{16,145},{17,144},{32,161},{33,160},{48,177},{49,1... | collective-permute-start | bytes 98312 | tf_op jit(solution)/shard_map/ppermute | solution.py:273
  2.2 0.8 %convert_element_type.3 = bf16[64,64]{1,0:T(8,128)(2,1)S(1)} convert(f32[64,64]{1,0:T(8,128)} %unit_ref.1) | non-fusion elementwise | flops 4096 | bytes 24576 | tf_op jit(solution)/shard_map/convert_element_type | solution.py:283
  3.0 0.1 pad_maximum_fusion
  3.1 0.7 %broadcast_in_dim.3 = bf16[16,32,128]{2,1,0:T(8,128)(2,1)} broadcast(bf16[32,128]{1,0:T(8,128)(2,1)S(1)} %pad_maximum_fusion), dimensions={1,2} | broadcast | bytes 139264 | tf_op jit(solution)/shard_map/broadcast_in_dim | solution.py:283
  3.7 9.1 %all-to-all-start = ((bf16[16,32,128]{2,1,0:T(8,128)(2,1)}), bf16[16,32,128]{2,1,0:T(8,128)(2,1)S(1)}, u32[]{:S(2)}, u32[]{:S(2)}) async-start(bf16[16,32,128]{2,1,0:T(8,128)(2,1)} %broadcast_in_dim.3), calls=%async_computation | async-start | bytes 262144 | tf_op jit(solution)/shard_map/all_to_all | solution.py:284
  12.8 0.0 collective-permute-done.other_ref
  12.9 3.8 %by_unit.1 = (bf16[5,1024,256]{2,1,0:T(8,128)(2,1)S(1)}, f32[64,1024]{1,0:T(8,128)S(1)}, f32[64,256]{1,0:T(8,128)S(1)}, bf16[16,128]{1,0:T(8,128)(2,1)S(1)}, f32[16,64]{1,0:T(8,128)S(1)}) custom-call(bf16[16,1024,256]{2,1,0:T(8,128)(2,1)} %tensor_far.3, f32[64,128]{1,0:T(8,128)S(1)} %collective-permute-done.other_ref, f32[64,128]{1,0:T(8,128)} %bitcast.3, ...), custom_call_target="tpu_custom_call" | custom-call | flops 8589934592 | bytes 8388608 | tf_op jit(solution)/shard_map/by_unit/pallas_call | solution.py:27
  16.7 7.3 %all-to-all-done.gather_ref = bf16[16,32,128]{2,1,0:T(8,128)(2,1)S(1)} async-done(((bf16[16,32,128]{2,1,0:T(8,128)(2,1)}), bf16[16,32,128]{2,1,0:T(8,128)(2,1)S(1)}, u32[]{:S(2)}, u32[]{:S(2)}) %all-to-all-start) | async-done | bytes 131104 | tf_op jit(solution)/shard_map/all_to_all | solution.py:284
  24.0 5.1 %by_feature.1 = (bf16[208,128]{1,0:T(8,128)(2,1)S(1)}, bf16[8,32,128]{2,1,0:T(8,128)(2,1)S(1)}, f32[8,32,128]{2,1,0:T(8,128)S(1)}) custom-call(bf16[16,1024,256]{2,1,0:T(8,128)(2,1)} %tensor_far.3, bf16[5,1024,256]{2,1,0:T(8,128)(2,1)S(1)} %get-tuple-element.21.kept_ref, bf16[16,32,128]{2,1,0:T(8,128)(2,1)S(1)} %all-to-all-done.gather_ref, ...), custom_call_target="tpu_custom_call" | custom-call | flops 8589934592 | bytes 8388608 | tf_op jit(solution)/shard_map/by_feature/pallas_call | solution.py:27
  29.1 0.1 collective-permute-start.1
  29.2 0.8 %collective-permute-start.3 = (bf16[8,32,128]{2,1,0:T(8,128)(2,1)S(1)}, bf16[8,32,128]{2,1,0:T(8,128)(2,1)S(1)}, u32[]{:S(2)}, u32[]{:S(2)}) collective-permute-start(bf16[8,32,128]{2,1,0:T(8,128)(2,1)S(1)} %get-tuple-element.27), channel_id=1, source_target_pairs={{0,1},{1,0},{2,3},{3,2},{4,5},{5,4},{6,7},{7,6},{8,9},{9,8},{10,11... | collective-permute-start | bytes 196616 | tf_op jit(solution)/shard_map/ppermute | solution.py:325
  30.0 0.4 collective-permute-done.1.s1
  30.5 1.7 %collective-permute-start.2 = (bf16[208,128]{1,0:T(8,128)(2,1)S(1)}, bf16[208,128]{1,0:T(8,128)(2,1)S(1)}, u32[]{:S(2)}, u32[]{:S(2)}) collective-permute-start(bf16[208,128]{1,0:T(8,128)(2,1)S(1)} %pair_sums.1.s0), channel_id=1, source_target_pairs={{0,32},{16,48},{32,0},{48,16},{64,96},{80,112},{96,64},{112,80},{1... | collective-permute-start | bytes 159752 | tf_op jit(solution)/shard_map/ppermute | solution.py:268
  32.1 3.1 %collective-permute-done.3.other_unit_ref = bf16[8,32,128]{2,1,0:T(8,128)(2,1)S(1)} collective-permute-done((bf16[8,32,128]{2,1,0:T(8,128)(2,1)S(1)}, bf16[8,32,128]{2,1,0:T(8,128)(2,1)S(1)}, u32[]{:S(2)}, u32[]{:S(2)}) %collective-permute-start.3) | collective-permute-done | bytes 65568 | tf_op jit(solution)/shard_map/ppermute | solution.py:325
  35.2 0.0 collective-permute-done.2.s1
  35.2 0.7 %near_sums.1 = (bf16[8,64,128]{2,1,0:T(8,128)(2,1)}, f32[72,128]{1,0:T(8,128)S(1)}, f32[96,128]{1,0:T(8,128)S(1)}) custom-call(bf16[208,128]{1,0:T(8,128)(2,1)S(1)} %pair_sums.1.s0, bf16[208,128]{1,0:T(8,128)(2,1)S(1)} %collective-permute-done.2.s1, f32[8,32,128]{2,1,0:T(8,128)S(1)} %get-tuple-element.26.by_unit_ref, ...), custom_call_target="tpu_custom_call" | custom-call | tf_op jit(solution)/shard_map/near_sums/pallas_call | solution.py:27
  35.9 3.4 %all-to-all-start.1 = ((bf16[8,64,128]{2,1,0:T(8,128)(2,1)}), bf16[8,64,128]{2,1,0:T(8,128)(2,1)S(1)}, u32[]{:S(2)}, u32[]{:S(2)}) async-start(bf16[8,64,128]{2,1,0:T(8,128)(2,1)} %get-tuple-element.29), calls=%async_computation.1 | async-start | bytes 262144 | tf_op jit(solution)/shard_map/all_to_all | solution.py:334
  39.3 1.4 %collective-permute-start.4 = (f32[72,128]{1,0:T(8,128)S(1)}, f32[72,128]{1,0:T(8,128)S(1)}, u32[]{:S(2)}, u32[]{:S(2)}) collective-permute-start(f32[72,128]{1,0:T(8,128)S(1)} %get-tuple-element.31), channel_id=1, source_target_pairs={{0,129},{1,128},{16,145},{17,144},{32,161},{33,160},{48,177},{49,1... | collective-permute-start | bytes 110600 | tf_op jit(solution)/shard_map/ppermute | solution.py:273
  40.6 2.7 %collective-permute-done.4.other_ref = f32[72,128]{1,0:T(8,128)S(1)} collective-permute-done((f32[72,128]{1,0:T(8,128)S(1)}, f32[72,128]{1,0:T(8,128)S(1)}, u32[]{:S(2)}, u32[]{:S(2)}) %collective-permute-start.4) | collective-permute-done | bytes 36896 | tf_op jit(solution)/shard_map/ppermute | solution.py:273
  43.3 0.3 other_sums.1
  43.6 4.7 %all-to-all-done.1.scatter_ref = bf16[8,64,128]{2,1,0:T(8,128)(2,1)S(1)} async-done(((bf16[8,64,128]{2,1,0:T(8,128)(2,1)}), bf16[8,64,128]{2,1,0:T(8,128)(2,1)S(1)}, u32[]{:S(2)}, u32[]{:S(2)}) %all-to-all-start.1) | async-done | bytes 131104 | tf_op jit(solution)/shard_map/all_to_all | solution.py:334
  48.4 0.2 group_sums.1
  48.5 3.9 %collective-permute-start.7 = (bf16[160,128]{1,0:T(8,128)(2,1)S(1)}, bf16[160,128]{1,0:T(8,128)(2,1)S(1)}, u32[]{:S(2)}, u32[]{:S(2)}) collective-permute-start(bf16[160,128]{1,0:T(8,128)(2,1)S(1)} %get-tuple-element.33.s0), channel_id=1, source_target_pairs={{0,224},{16,240},{32,192},{48,208},{64,160},{80,176},{96,128},{112... | collective-permute-start | bytes 122888 | tf_op jit(solution)/shard_map/ppermute | solution.py:268
  52.5 0.2 collective-permute-start.6
  52.7 0.5 collective-permute-start.5
  53.2 1.5 %collective-permute-done.7.s3 = bf16[160,128]{1,0:T(8,128)(2,1)S(1)} collective-permute-done((bf16[160,128]{1,0:T(8,128)(2,1)S(1)}, bf16[160,128]{1,0:T(8,128)(2,1)S(1)}, u32[]{:S(2)}, u32[]{:S(2)}) %collective-permute-start.7) | collective-permute-done | bytes 40992 | tf_op jit(solution)/shard_map/ppermute | solution.py:268
  54.7 3.0 %collective-permute-done.6.s2 = bf16[160,128]{1,0:T(8,128)(2,1)S(1)} collective-permute-done((bf16[160,128]{1,0:T(8,128)(2,1)S(1)}, bf16[160,128]{1,0:T(8,128)(2,1)S(1)}, u32[]{:S(2)}, u32[]{:S(2)}) %collective-permute-start.6) | collective-permute-done | bytes 40992 | tf_op jit(solution)/shard_map/ppermute | solution.py:268
  57.7 0.0 collective-permute-done.5.s1
  57.7 0.0 copy-done
  57.7 0.0 copy-done.1
  57.7 0.0 copy-done.2
  57.7 0.9 %gradients.1 = (f32[64,64]{1,0:T(8,128)}, f32[16,64]{1,0:T(8,128)}, f32[64,128]{1,0:T(8,128)}) custom-call(bf16[160,128]{1,0:T(8,128)(2,1)S(1)} %get-tuple-element.33.s0, bf16[160,128]{1,0:T(8,128)(2,1)S(1)} %collective-permute-done.5.s1, bf16[160,128]{1,0:T(8,128)(2,1)S(1)} %collective-permute-done.6.s2, bf16[160,128]{1,0:T(8,128)(2,1)S(1)} %collective-permute-done.7.s3, ...), custom_call_target="tpu_custom_call" | custom-call | tf_op jit(solution)/shard_map/gradients/pallas_call | solution.py:27
  (5 shorter events, 0.0 us)
Async XLA Ops:
  0.6 12.2 %collective-permute-start = (f32[64,128]{1,0:T(8,128)}, f32[64,128]{1,0:T(8,128)S(1)}, u32[]{:S(2)}, u32[]{:S(2)}) collective-permute-start(f32[64,128]{1,0:T(8,128)} %bitcast.2), channel_id=1, source_target_pairs={{0,129},{1,128},{16,145},{17,144},{32,161},{33,160},{48,177},{49,1... | collective-permute-start | bytes 98312 | tf_op jit(solution)/shard_map/ppermute | solution.py:273
  3.7 20.2 %all-to-all-start = ((bf16[16,32,128]{2,1,0:T(8,128)(2,1)}), bf16[16,32,128]{2,1,0:T(8,128)(2,1)S(1)}, u32[]{:S(2)}, u32[]{:S(2)}) async-start(bf16[16,32,128]{2,1,0:T(8,128)(2,1)} %broadcast_in_dim.3), calls=%async_computation | async-start | bytes 262144 | tf_op jit(solution)/shard_map/all_to_all | solution.py:284
  24.0 33.7 %copy-start = (f32[64,64]{1,0:T(8,128)S(1)}, f32[64,64]{1,0:T(8,128)}, u32[]{:S(2)}) copy-start(f32[64,64]{1,0:T(8,128)} %unit_ref.1) | copy-start | bytes 49156
  24.0 33.7 %copy-start.1 = (f32[128,64]{0,1:T(8,128)S(1)}, f32[128,64]{0,1:T(8,128)}, u32[]{:S(2)}) copy-start(f32[128,64]{0,1:T(8,128)} %param.7) | copy-start | bytes 98308
  24.0 33.7 %copy-start.2 = (f32[16,64]{1,0:T(8,128)S(1)}, f32[16,64]{1,0:T(8,128)}, u32[]{:S(2)}) copy-start(f32[16,64]{1,0:T(8,128)} %window_ref.1) | copy-start | bytes 12292
  29.1 1.3 %collective-permute-start.1 = (bf16[208,128]{1,0:T(8,128)(2,1)S(1)}, bf16[208,128]{1,0:T(8,128)(2,1)S(1)}, u32[]{:S(2)}, u32[]{:S(2)}) collective-permute-start(bf16[208,128]{1,0:T(8,128)(2,1)S(1)} %get-tuple-element.25.s0), channel_id=1, source_target_pairs={{0,16},{16,0},{32,48},{48,32},{64,80},{80,64},{96,112},{112,96},{1... | collective-permute-start | bytes 159752 | tf_op jit(solution)/shard_map/ppermute | solution.py:268
  29.2 6.0 %collective-permute-start.3 = (bf16[8,32,128]{2,1,0:T(8,128)(2,1)S(1)}, bf16[8,32,128]{2,1,0:T(8,128)(2,1)S(1)}, u32[]{:S(2)}, u32[]{:S(2)}) collective-permute-start(bf16[8,32,128]{2,1,0:T(8,128)(2,1)S(1)} %get-tuple-element.27), channel_id=1, source_target_pairs={{0,1},{1,0},{2,3},{3,2},{4,5},{5,4},{6,7},{7,6},{8,9},{9,8},{10,11... | collective-permute-start | bytes 196616 | tf_op jit(solution)/shard_map/ppermute | solution.py:325
  30.5 4.8 %collective-permute-start.2 = (bf16[208,128]{1,0:T(8,128)(2,1)S(1)}, bf16[208,128]{1,0:T(8,128)(2,1)S(1)}, u32[]{:S(2)}, u32[]{:S(2)}) collective-permute-start(bf16[208,128]{1,0:T(8,128)(2,1)S(1)} %pair_sums.1.s0), channel_id=1, source_target_pairs={{0,32},{16,48},{32,0},{48,16},{64,96},{80,112},{96,64},{112,80},{1... | collective-permute-start | bytes 159752 | tf_op jit(solution)/shard_map/ppermute | solution.py:268
  35.9 12.5 %all-to-all-start.1 = ((bf16[8,64,128]{2,1,0:T(8,128)(2,1)}), bf16[8,64,128]{2,1,0:T(8,128)(2,1)S(1)}, u32[]{:S(2)}, u32[]{:S(2)}) async-start(bf16[8,64,128]{2,1,0:T(8,128)(2,1)} %get-tuple-element.29), calls=%async_computation.1 | async-start | bytes 262144 | tf_op jit(solution)/shard_map/all_to_all | solution.py:334
  39.3 4.0 %collective-permute-start.4 = (f32[72,128]{1,0:T(8,128)S(1)}, f32[72,128]{1,0:T(8,128)S(1)}, u32[]{:S(2)}, u32[]{:S(2)}) collective-permute-start(f32[72,128]{1,0:T(8,128)S(1)} %get-tuple-element.31), channel_id=1, source_target_pairs={{0,129},{1,128},{16,145},{17,144},{32,161},{33,160},{48,177},{49,1... | collective-permute-start | bytes 110600 | tf_op jit(solution)/shard_map/ppermute | solution.py:273
  48.5 6.2 %collective-permute-start.7 = (bf16[160,128]{1,0:T(8,128)(2,1)S(1)}, bf16[160,128]{1,0:T(8,128)(2,1)S(1)}, u32[]{:S(2)}, u32[]{:S(2)}) collective-permute-start(bf16[160,128]{1,0:T(8,128)(2,1)S(1)} %get-tuple-element.33.s0), channel_id=1, source_target_pairs={{0,224},{16,240},{32,192},{48,208},{64,160},{80,176},{96,128},{112... | collective-permute-start | bytes 122888 | tf_op jit(solution)/shard_map/ppermute | solution.py:268
  52.5 5.2 %collective-permute-start.6 = (bf16[160,128]{1,0:T(8,128)(2,1)S(1)}, bf16[160,128]{1,0:T(8,128)(2,1)S(1)}, u32[]{:S(2)}, u32[]{:S(2)}) collective-permute-start(bf16[160,128]{1,0:T(8,128)(2,1)S(1)} %get-tuple-element.33.s0), channel_id=1, source_target_pairs={{0,96},{16,112},{32,64},{48,80},{64,32},{80,48},{96,0},{112,16},{1... | collective-permute-start | bytes 122888 | tf_op jit(solution)/shard_map/ppermute | solution.py:268
  52.7 5.0 %collective-permute-start.5 = (bf16[160,128]{1,0:T(8,128)(2,1)S(1)}, bf16[160,128]{1,0:T(8,128)(2,1)S(1)}, u32[]{:S(2)}, u32[]{:S(2)}) collective-permute-start(bf16[160,128]{1,0:T(8,128)(2,1)S(1)} %get-tuple-element.33.s0), channel_id=1, source_target_pairs={{0,128},{16,144},{32,160},{48,176},{64,192},{80,208},{96,224},{112... | collective-permute-start | bytes 122888 | tf_op jit(solution)/shard_map/ppermute | solution.py:268

commit v4 on v3

--- a/solution.py
+++ b/solution.py
@@ -14,6 +14,7 @@
 NT = (((1,), (1,)), ((), ()))
 TN = (((0,), (0,)), ((), ()))
 GROUP = ("feat", "tm")
+ORDER = [*range(12, 16), *range(12)]
 FAR = (8, 6, 14)
 VMEM = pl.BlockSpec(memory_space=pltpu.VMEM)
 HBM = pl.BlockSpec(memory_space=pltpu.HBM)
@@ -146,7 +147,7 @@
     start(copies[0:4])
     left = lax.broadcasted_iota(jnp.int32, (32, 128), 1) < 64
     for at in range(0, 16, 2):
-        rows = [stack(gather_ref[at].astype(F32)), stack(gather_ref[at + 1].astype(F32))]
+        rows = [stack(gather_ref[ORDER.index(at + k)].astype(F32)) for k in range(2)]
         unit_ref[:, pl.ds(at * 64, 128)] = jnp.concatenate(rows, axis=0).T.astype(BF16)
     start(copies[4:8])
     unit = unit_ref[...]
@@ -281,7 +282,7 @@
     shape = jax.ShapeDtypeStruct
     feat = feat_factor.T
     gather = jnp.broadcast_to(spread(unit_factor.astype(BF16)), (16, 32, 128))
-    gather = lax.all_to_all(gather.reshape(512, 128), GROUP, 0, 0, tiled=True).reshape(16, 32, 128)
+    gather = lax.all_to_all(gather.reshape(512, 128), GROUP, 0, 0, tiled=True, axis_index_groups=[ORDER]).reshape(16, 32, 128)
     cost = pl.CostEstimate(flops=2**33, bytes_accessed=2**23, transcendentals=0)
     kept, early = 5, 8
     slabs = functools.partial(pltpu.VMEM, dtype=BF16)

time: 59 us -> 58 us (0.983)
  waiting for transfers between devices: 22.7 us -> 19.5 us
  starting transfers between devices: 22.7 us -> 24.9 us
    all_to_all x1, waiting for transfers between devices: 7.28 us -> 4.02 us  [body(): lax.all_to_all(gather.reshape(512, 128), GROUP, 0, 0, tiled=True, axis_in...]
    all_to_all x1, starting transfers between devices: 3.37 us -> 4.85 us  [body(): lax.all_to_all(scatter.reshape(512, 128), 'feat', 0, 0, tiled=True)]
where the time goes in v4:
time: 58 us; the launch traced here: 57.6 us
  starting transfers between devices  24.9 us (43%)
  waiting for transfers between devices  19.5 us (34%)
  Pallas kernels  11 us (19%)
  other arithmetic  0.84 us (1%)
  between operations  0.69 us (1%)
  local copies, waits for them, and re-layouts  0.68 us (1%)
    pallas_call x7, Pallas kernels, call(): pl.pallas_call(kernel, out_shape=out_shape, in_specs=[HBM if at in far el...  11 us
    all_to_all x1, starting transfers between devices, body(): lax.all_to_all(gather.reshape(512, 128), GROUP, 0, 0, tiled=True, axis_in...  9.62 us
    ppermute x5, starting transfers between devices, by_xor(): return lax.ppermute(value, 'unit', [(i, i ^ mask) for i in range(count)])  6.67 us
    ppermute x5, waiting for transfers between devices, by_xor(): return lax.ppermute(value, 'unit', [(i, i ^ mask) for i in range(count)])  5.2 us
    all_to_all x1, starting transfers between devices, body(): lax.all_to_all(scatter.reshape(512, 128), 'feat', 0, 0, tiled=True)  4.85 us
    all_to_all x1, waiting for transfers between devices, body(): lax.all_to_all(scatter.reshape(512, 128), 'feat', 0, 0, tiled=True)  4.83 us
    all_to_all x1, waiting for transfers between devices, body(): lax.all_to_all(gather.reshape(512, 128), GROUP, 0, 0, tiled=True, axis_in...  4.02 us
    ppermute x2, starting transfers between devices, other_windows(): lax.ppermute(value, ('unit', 'tm'), [(i, i ^ 17) for i in range(count)])  3.16 us
  transfers between devices with their start and end apart: 10, of which 7 were waited for; matrix products, arithmetic and copies ran while one was open for 3% of the time, Pallas kernels for 7%

profile of v4, /device:TPU:2, one launch (start us, length us, event | category | flops | bytes accessed | tf_op | source)
XLA Modules:
  0.0 57.6 jit_solution(2409014003468601939)
XLA Ops:
  0.6 1.6 %collective-permute-start = (f32[64,128]{1,0:T(8,128)}, f32[64,128]{1,0:T(8,128)S(1)}, u32[]{:S(2)}, u32[]{:S(2)}) collective-permute-start(f32[64,128]{1,0:T(8,128)} %bitcast.2), channel_id=1, source_target_pairs={{0,129},{1,128},{16,145},{17,144},{32,161},{33,160},{48,177},{49,1... | collective-permute-start | bytes 98312 | tf_op jit(solution)/shard_map/ppermute | solution.py:274
  2.2 0.8 %convert_element_type.3 = bf16[64,64]{1,0:T(8,128)(2,1)S(1)} convert(f32[64,64]{1,0:T(8,128)} %unit_ref.1) | non-fusion elementwise | flops 4096 | bytes 24576 | tf_op jit(solution)/shard_map/convert_element_type | solution.py:284
  3.0 0.1 pad_maximum_fusion
  3.1 0.7 %broadcast_in_dim.3 = bf16[16,32,128]{2,1,0:T(8,128)(2,1)} broadcast(bf16[32,128]{1,0:T(8,128)(2,1)S(1)} %pad_maximum_fusion), dimensions={1,2} | broadcast | bytes 139264 | tf_op jit(solution)/shard_map/broadcast_in_dim | solution.py:284
  3.7 9.6 %all-to-all-start = ((bf16[16,32,128]{2,1,0:T(8,128)(2,1)}), bf16[16,32,128]{2,1,0:T(8,128)(2,1)S(1)}, u32[]{:S(2)}, u32[]{:S(2)}) async-start(bf16[16,32,128]{2,1,0:T(8,128)(2,1)} %broadcast_in_dim.3), calls=%async_computation | async-start | bytes 262144 | tf_op jit(solution)/shard_map/all_to_all | solution.py:285
  13.3 0.0 collective-permute-done.other_ref
  13.3 3.8 %by_unit.1 = (bf16[5,1024,256]{2,1,0:T(8,128)(2,1)S(1)}, f32[64,1024]{1,0:T(8,128)S(1)}, f32[64,256]{1,0:T(8,128)S(1)}, bf16[16,128]{1,0:T(8,128)(2,1)S(1)}, f32[16,64]{1,0:T(8,128)S(1)}) custom-call(bf16[16,1024,256]{2,1,0:T(8,128)(2,1)} %tensor_far.3, f32[64,128]{1,0:T(8,128)S(1)} %collective-permute-done.other_ref, f32[64,128]{1,0:T(8,128)} %bitcast.3, ...), custom_call_target="tpu_custom_call" | custom-call | flops 8589934592 | bytes 8388608 | tf_op jit(solution)/shard_map/by_unit/pallas_call | solution.py:28
  17.2 4.0 %all-to-all-done.gather_ref = bf16[16,32,128]{2,1,0:T(8,128)(2,1)S(1)} async-done(((bf16[16,32,128]{2,1,0:T(8,128)(2,1)}), bf16[16,32,128]{2,1,0:T(8,128)(2,1)S(1)}, u32[]{:S(2)}, u32[]{:S(2)}) %all-to-all-start) | async-done | bytes 131104 | tf_op jit(solution)/shard_map/all_to_all | solution.py:285
  21.2 5.1 %by_feature.1 = (bf16[208,128]{1,0:T(8,128)(2,1)S(1)}, bf16[8,32,128]{2,1,0:T(8,128)(2,1)S(1)}, f32[8,32,128]{2,1,0:T(8,128)S(1)}) custom-call(bf16[16,1024,256]{2,1,0:T(8,128)(2,1)} %tensor_far.3, bf16[5,1024,256]{2,1,0:T(8,128)(2,1)S(1)} %get-tuple-element.21.kept_ref, bf16[16,32,128]{2,1,0:T(8,128)(2,1)S(1)} %all-to-all-done.gather_ref, ...), custom_call_target="tpu_custom_call" | custom-call | flops 8589934592 | bytes 8388608 | tf_op jit(solution)/shard_map/by_feature/pallas_call | solution.py:28
  26.3 0.1 collective-permute-start.1
  26.4 0.6 collective-permute-start.3
  27.0 0.7 %collective-permute-done.1.s1 = bf16[208,128]{1,0:T(8,128)(2,1)S(1)} collective-permute-done((bf16[208,128]{1,0:T(8,128)(2,1)S(1)}, bf16[208,128]{1,0:T(8,128)(2,1)S(1)}, u32[]{:S(2)}, u32[]{:S(2)}) %collective-permute-start.1) | collective-permute-done | bytes 53280 | tf_op jit(solution)/shard_map/ppermute | solution.py:269
  27.7 1.7 %collective-permute-start.2 = (bf16[208,128]{1,0:T(8,128)(2,1)S(1)}, bf16[208,128]{1,0:T(8,128)(2,1)S(1)}, u32[]{:S(2)}, u32[]{:S(2)}) collective-permute-start(bf16[208,128]{1,0:T(8,128)(2,1)S(1)} %pair_sums.1.s0), channel_id=1, source_target_pairs={{0,32},{16,48},{32,0},{48,16},{64,96},{80,112},{96,64},{112,80},{1... | collective-permute-start | bytes 159752 | tf_op jit(solution)/shard_map/ppermute | solution.py:269
  29.4 3.1 %collective-permute-done.3.other_unit_ref = bf16[8,32,128]{2,1,0:T(8,128)(2,1)S(1)} collective-permute-done((bf16[8,32,128]{2,1,0:T(8,128)(2,1)S(1)}, bf16[8,32,128]{2,1,0:T(8,128)(2,1)S(1)}, u32[]{:S(2)}, u32[]{:S(2)}) %collective-permute-start.3) | collective-permute-done | bytes 65568 | tf_op jit(solution)/shard_map/ppermute | solution.py:326
  32.5 0.0 collective-permute-done.2.s1
  32.5 0.7 %near_sums.1 = (bf16[8,64,128]{2,1,0:T(8,128)(2,1)}, f32[72,128]{1,0:T(8,128)S(1)}, f32[96,128]{1,0:T(8,128)S(1)}) custom-call(bf16[208,128]{1,0:T(8,128)(2,1)S(1)} %pair_sums.1.s0, bf16[208,128]{1,0:T(8,128)(2,1)S(1)} %collective-permute-done.2.s1, f32[8,32,128]{2,1,0:T(8,128)S(1)} %get-tuple-element.26.by_unit_ref, ...), custom_call_target="tpu_custom_call" | custom-call | tf_op jit(solution)/shard_map/near_sums/pallas_call | solution.py:28
  33.1 4.9 %all-to-all-start.1 = ((bf16[8,64,128]{2,1,0:T(8,128)(2,1)}), bf16[8,64,128]{2,1,0:T(8,128)(2,1)S(1)}, u32[]{:S(2)}, u32[]{:S(2)}) async-start(bf16[8,64,128]{2,1,0:T(8,128)(2,1)} %get-tuple-element.29), calls=%async_computation.1 | async-start | bytes 262144 | tf_op jit(solution)/shard_map/all_to_all | solution.py:335
  38.0 1.6 %collective-permute-start.4 = (f32[72,128]{1,0:T(8,128)S(1)}, f32[72,128]{1,0:T(8,128)S(1)}, u32[]{:S(2)}, u32[]{:S(2)}) collective-permute-start(f32[72,128]{1,0:T(8,128)S(1)} %get-tuple-element.31), channel_id=1, source_target_pairs={{0,129},{1,128},{16,145},{17,144},{32,161},{33,160},{48,177},{49,1... | collective-permute-start | bytes 110600 | tf_op jit(solution)/shard_map/ppermute | solution.py:274
  39.6 2.4 %collective-permute-done.4.other_ref = f32[72,128]{1,0:T(8,128)S(1)} collective-permute-done((f32[72,128]{1,0:T(8,128)S(1)}, f32[72,128]{1,0:T(8,128)S(1)}, u32[]{:S(2)}, u32[]{:S(2)}) %collective-permute-start.4) | collective-permute-done | bytes 36896 | tf_op jit(solution)/shard_map/ppermute | solution.py:274
  42.0 0.3 other_sums.1
  42.2 4.8 %all-to-all-done.1.scatter_ref = bf16[8,64,128]{2,1,0:T(8,128)(2,1)S(1)} async-done(((bf16[8,64,128]{2,1,0:T(8,128)(2,1)}), bf16[8,64,128]{2,1,0:T(8,128)(2,1)S(1)}, u32[]{:S(2)}, u32[]{:S(2)}) %all-to-all-start.1) | async-done | bytes 131104 | tf_op jit(solution)/shard_map/all_to_all | solution.py:335
  47.1 0.2 group_sums.1
  47.2 4.3 %collective-permute-start.7 = (bf16[160,128]{1,0:T(8,128)(2,1)S(1)}, bf16[160,128]{1,0:T(8,128)(2,1)S(1)}, u32[]{:S(2)}, u32[]{:S(2)}) collective-permute-start(bf16[160,128]{1,0:T(8,128)(2,1)S(1)} %get-tuple-element.33.s0), channel_id=1, source_target_pairs={{0,224},{16,240},{32,192},{48,208},{64,160},{80,176},{96,128},{112... | collective-permute-start | bytes 122888 | tf_op jit(solution)/shard_map/ppermute | solution.py:269
  51.5 0.2 collective-permute-start.6
  51.7 0.4 collective-permute-start.5
  52.2 1.4 %collective-permute-done.7.s3 = bf16[160,128]{1,0:T(8,128)(2,1)S(1)} collective-permute-done((bf16[160,128]{1,0:T(8,128)(2,1)S(1)}, bf16[160,128]{1,0:T(8,128)(2,1)S(1)}, u32[]{:S(2)}, u32[]{:S(2)}) %collective-permute-start.7) | collective-permute-done | bytes 40992 | tf_op jit(solution)/shard_map/ppermute | solution.py:269
  53.5 3.2 %collective-permute-done.6.s2 = bf16[160,128]{1,0:T(8,128)(2,1)S(1)} collective-permute-done((bf16[160,128]{1,0:T(8,128)(2,1)S(1)}, bf16[160,128]{1,0:T(8,128)(2,1)S(1)}, u32[]{:S(2)}, u32[]{:S(2)}) %collective-permute-start.6) | collective-permute-done | bytes 40992 | tf_op jit(solution)/shard_map/ppermute | solution.py:269
  56.7 0.0 collective-permute-done.5.s1
  56.7 0.0 copy-done
  56.7 0.0 copy-done.1
  56.7 0.0 copy-done.2
  56.7 0.9 %gradients.1 = (f32[64,64]{1,0:T(8,128)}, f32[16,64]{1,0:T(8,128)}, f32[64,128]{1,0:T(8,128)}) custom-call(bf16[160,128]{1,0:T(8,128)(2,1)S(1)} %get-tuple-element.33.s0, bf16[160,128]{1,0:T(8,128)(2,1)S(1)} %collective-permute-done.5.s1, bf16[160,128]{1,0:T(8,128)(2,1)S(1)} %collective-permute-done.6.s2, bf16[160,128]{1,0:T(8,128)(2,1)S(1)} %collective-permute-done.7.s3, ...), custom_call_target="tpu_custom_call" | custom-call | tf_op jit(solution)/shard_map/gradients/pallas_call | solution.py:28
  (5 shorter events, 0.0 us)
Async XLA Ops:
  0.6 12.7 %collective-permute-start = (f32[64,128]{1,0:T(8,128)}, f32[64,128]{1,0:T(8,128)S(1)}, u32[]{:S(2)}, u32[]{:S(2)}) collective-permute-start(f32[64,128]{1,0:T(8,128)} %bitcast.2), channel_id=1, source_target_pairs={{0,129},{1,128},{16,145},{17,144},{32,161},{33,160},{48,177},{49,1... | collective-permute-start | bytes 98312 | tf_op jit(solution)/shard_map/ppermute | solution.py:274
  3.7 17.5 %all-to-all-start = ((bf16[16,32,128]{2,1,0:T(8,128)(2,1)}), bf16[16,32,128]{2,1,0:T(8,128)(2,1)S(1)}, u32[]{:S(2)}, u32[]{:S(2)}) async-start(bf16[16,32,128]{2,1,0:T(8,128)(2,1)} %broadcast_in_dim.3), calls=%async_computation | async-start | bytes 262144 | tf_op jit(solution)/shard_map/all_to_all | solution.py:285
  21.2 35.5 %copy-start = (f32[64,64]{1,0:T(8,128)S(1)}, f32[64,64]{1,0:T(8,128)}, u32[]{:S(2)}) copy-start(f32[64,64]{1,0:T(8,128)} %unit_ref.1) | copy-start | bytes 49156
  21.2 35.5 %copy-start.1 = (f32[128,64]{0,1:T(8,128)S(1)}, f32[128,64]{0,1:T(8,128)}, u32[]{:S(2)}) copy-start(f32[128,64]{0,1:T(8,128)} %param.7) | copy-start | bytes 98308
  21.2 35.5 %copy-start.2 = (f32[16,64]{1,0:T(8,128)S(1)}, f32[16,64]{1,0:T(8,128)}, u32[]{:S(2)}) copy-start(f32[16,64]{1,0:T(8,128)} %window_ref.1) | copy-start | bytes 12292
  26.3 1.3 %collective-permute-start.1 = (bf16[208,128]{1,0:T(8,128)(2,1)S(1)}, bf16[208,128]{1,0:T(8,128)(2,1)S(1)}, u32[]{:S(2)}, u32[]{:S(2)}) collective-permute-start(bf16[208,128]{1,0:T(8,128)(2,1)S(1)} %get-tuple-element.25.s0), channel_id=1, source_target_pairs={{0,16},{16,0},{32,48},{48,32},{64,80},{80,64},{96,112},{112,96},{1... | collective-permute-start | bytes 159752 | tf_op jit(solution)/shard_map/ppermute | solution.py:269
  26.4 6.0 %collective-permute-start.3 = (bf16[8,32,128]{2,1,0:T(8,128)(2,1)S(1)}, bf16[8,32,128]{2,1,0:T(8,128)(2,1)S(1)}, u32[]{:S(2)}, u32[]{:S(2)}) collective-permute-start(bf16[8,32,128]{2,1,0:T(8,128)(2,1)S(1)} %get-tuple-element.27), channel_id=1, source_target_pairs={{0,1},{1,0},{2,3},{3,2},{4,5},{5,4},{6,7},{7,6},{8,9},{9,8},{10,11... | collective-permute-start | bytes 196616 | tf_op jit(solution)/shard_map/ppermute | solution.py:326
  27.7 4.8 %collective-permute-start.2 = (bf16[208,128]{1,0:T(8,128)(2,1)S(1)}, bf16[208,128]{1,0:T(8,128)(2,1)S(1)}, u32[]{:S(2)}, u32[]{:S(2)}) collective-permute-start(bf16[208,128]{1,0:T(8,128)(2,1)S(1)} %pair_sums.1.s0), channel_id=1, source_target_pairs={{0,32},{16,48},{32,0},{48,16},{64,96},{80,112},{96,64},{112,80},{1... | collective-permute-start | bytes 159752 | tf_op jit(solution)/shard_map/ppermute | solution.py:269
  33.1 13.9 %all-to-all-start.1 = ((bf16[8,64,128]{2,1,0:T(8,128)(2,1)}), bf16[8,64,128]{2,1,0:T(8,128)(2,1)S(1)}, u32[]{:S(2)}, u32[]{:S(2)}) async-start(bf16[8,64,128]{2,1,0:T(8,128)(2,1)} %get-tuple-element.29), calls=%async_computation.1 | async-start | bytes 262144 | tf_op jit(solution)/shard_map/all_to_all | solution.py:335
  38.0 4.0 %collective-permute-start.4 = (f32[72,128]{1,0:T(8,128)S(1)}, f32[72,128]{1,0:T(8,128)S(1)}, u32[]{:S(2)}, u32[]{:S(2)}) collective-permute-start(f32[72,128]{1,0:T(8,128)S(1)} %get-tuple-element.31), channel_id=1, source_target_pairs={{0,129},{1,128},{16,145},{17,144},{32,161},{33,160},{48,177},{49,1... | collective-permute-start | bytes 110600 | tf_op jit(solution)/shard_map/ppermute | solution.py:274
  47.2 6.3 %collective-permute-start.7 = (bf16[160,128]{1,0:T(8,128)(2,1)S(1)}, bf16[160,128]{1,0:T(8,128)(2,1)S(1)}, u32[]{:S(2)}, u32[]{:S(2)}) collective-permute-start(bf16[160,128]{1,0:T(8,128)(2,1)S(1)} %get-tuple-element.33.s0), channel_id=1, source_target_pairs={{0,224},{16,240},{32,192},{48,208},{64,160},{80,176},{96,128},{112... | collective-permute-start | bytes 122888 | tf_op jit(solution)/shard_map/ppermute | solution.py:269
  51.5 5.2 %collective-permute-start.6 = (bf16[160,128]{1,0:T(8,128)(2,1)S(1)}, bf16[160,128]{1,0:T(8,128)(2,1)S(1)}, u32[]{:S(2)}, u32[]{:S(2)}) collective-permute-start(bf16[160,128]{1,0:T(8,128)(2,1)S(1)} %get-tuple-element.33.s0), channel_id=1, source_target_pairs={{0,96},{16,112},{32,64},{48,80},{64,32},{80,48},{96,0},{112,16},{1... | collective-permute-start | bytes 122888 | tf_op jit(solution)/shard_map/ppermute | solution.py:269
  51.7 5.0 %collective-permute-start.5 = (bf16[160,128]{1,0:T(8,128)(2,1)S(1)}, bf16[160,128]{1,0:T(8,128)(2,1)S(1)}, u32[]{:S(2)}, u32[]{:S(2)}) collective-permute-start(bf16[160,128]{1,0:T(8,128)(2,1)S(1)} %get-tuple-element.33.s0), channel_id=1, source_target_pairs={{0,128},{16,144},{32,160},{48,176},{64,192},{80,208},{96,224},{112... | collective-permute-start | bytes 122888 | tf_op jit(solution)/shard_map/ppermute | solution.py:269
